TPU v7x, 512 devices: a whole 4x4x16 slice. The times are simulated.
512 devices in a mesh: depth: 32 (over z, core), lat: 16 (over x, y).
Axes of the slice: x: 4, y: 4, z: 16, core: 2. Of those that a mesh axis runs over, the one named last changes fastest.
Arguments:
- checkpoint: float32 [9, 256, 256, 256], P(None, 'depth', 'lat'), may hold values from -6 to 6
- end_cotangent: float32 [9, 256, 256, 256], P(None, 'depth', 'lat'), may hold values from -6 to 6
- buoyancy: float32 [256, 256, 256], P('depth', 'lat'), may hold values from 0.15 to 0.4
- moduli: float32 [2, 256, 256, 256], P(None, 'depth', 'lat'), may hold values from 0.1 to 0.35
- yield_radius: float32 [256, 256, 256], P('depth', 'lat'), may hold values from 0.3 to 1.5
- mask: int32 [3, 256, 256, 256], P(None, 'depth', 'lat'), may hold values 0 or 1
- footprint: int32 [256, 256], P('lat'), may hold values from 0 to 63
- amplitude: float32 [64], replicated, may hold values from 0.5 to 2
Outputs:
- adjoint_state: float32 [9, 256, 256, 256], P(None, 'depth', 'lat')
- pulse_grad: float32 [64], replicated
All inputs are finite; a program needn't handle non-finite values. No bound on the sum of `mask` on one device may be relied on, other than what follows from the above.
Results may differ from a plain program's by a relative error of at most 0.00012.
Values sent between devices are 32-bit elements; how exact they have to be, the bound alone decides.
A program may use at most 64 MiB of HBM per device.

v0:
```python
import math

import jax
import jax.numpy as jnp
from jax import lax
from jax.sharding import PartitionSpec as P


def with_halo(block, sides, width):
    for axis, dim in sides:
        count = lax.axis_size(axis)
        forward = [(i, i + 1) for i in range(count - 1)]
        backward = [(target, source) for source, target in forward]
        low = lax.ppermute(
            lax.slice_in_dim(block, block.shape[dim] - width, None, axis=dim), axis, forward
        )
        high = lax.ppermute(lax.slice_in_dim(block, 0, width, axis=dim), axis, backward)
        block = jnp.concatenate([low, block, high], axis=dim)
    return block


def plus_z(field):
    return field[2:, 1:-1] - field[1:-1, 1:-1]


def minus_z(field):
    return field[1:-1, 1:-1] - field[:-2, 1:-1]


def plus_x(field):
    return field[1:-1, 2:] - field[1:-1, 1:-1]


def minus_x(field):
    return field[1:-1, 1:-1] - field[1:-1, :-2]


def plus_y(field):
    middle = field[1:-1, 1:-1]
    return jnp.concatenate([middle[..., 1:], jnp.zeros_like(middle[..., :1])], -1) - middle


def minus_y(field):
    middle = field[1:-1, 1:-1]
    return middle - jnp.concatenate([jnp.zeros_like(middle[..., :1]), middle[..., :-1]], -1)


def divergence(tensor):
    return jnp.stack(
        [
            plus_x(tensor[0]) + minus_y(tensor[3]) + minus_z(tensor[4]),
            minus_x(tensor[3]) + plus_y(tensor[1]) + minus_z(tensor[5]),
            minus_x(tensor[4]) + minus_y(tensor[5]) + plus_z(tensor[2]),
        ]
    )


def gradient(vector):
    return jnp.stack(
        [
            minus_x(vector[0]),
            minus_y(vector[1]),
            minus_z(vector[2]),
            plus_y(vector[0]) + plus_x(vector[1]),
            plus_z(vector[0]) + plus_x(vector[2]),
            plus_z(vector[1]) + plus_y(vector[2]),
        ]
    )


def radial_return(stress, strain, lame, shear, limit, plastic):
    trace = strain[0] + strain[1] + strain[2]
    normal = [stress[a] + lame * trace + 2.0 * shear * strain[a] for a in range(3)]
    sheared = [stress[a] + shear * strain[a] for a in range(3, 6)]
    mean = (normal[0] + normal[1] + normal[2]) / 3.0
    devs = [normal[a] - mean for a in range(3)]
    qsq = (
        devs[0] * devs[0]
        + devs[1] * devs[1]
        + devs[2] * devs[2]
        + 2.0 * (sheared[0] * sheared[0] + sheared[1] * sheared[1] + sheared[2] * sheared[2])
    )
    factor = 1.0 - plastic + plastic * limit / jnp.sqrt(limit * limit + qsq)
    return jnp.stack(
        [
            mean + factor * devs[0],
            mean + factor * devs[1],
            mean + factor * devs[2],
            factor * sheared[0],
            factor * sheared[1],
            factor * sheared[2],
        ]
    )


def coupled(tensor, vector, forward, buoyancy):
    wide_tensor = with_halo(tensor, (("depth", 1), ("lat", 2)), 1)
    if forward:
        moved = vector + buoyancy * divergence(wide_tensor)
        scaled = moved
    else:
        moved = vector - divergence(wide_tensor)
        scaled = buoyancy * moved
    wide_vector = with_halo(scaled, (("depth", 1), ("lat", 2)), 1)
    return (moved, gradient(wide_vector))


def per_device(
    checkpoint, end_cotangent, buoyancy, moduli, yield_radius, mask, footprint, amplitude
):
    steps = mask.shape[0]
    pulses = amplitude.shape[0]
    strip = checkpoint.shape[2]
    across = checkpoint.shape[3]
    lame = moduli[0]
    shear = moduli[1]
    is_top = (lax.axis_index("depth") == 0).astype(jnp.float32)
    onehot = (footprint.reshape(1, -1) == jnp.arange(pulses, dtype=jnp.int32)[:, None]).astype(
        jnp.float32
    )
    load_map = (
        jnp.dot(amplitude, onehot, precision=lax.Precision.HIGHEST).reshape(strip, across) * is_top
    )
    history = []
    state = checkpoint
    for index in range(steps):
        plastic = mask[index].astype(jnp.float32)
        velocity, strain = coupled(state[3:], state[:3], True, buoyancy)
        stress = radial_return(state[3:], strain, lame, shear, yield_radius, plastic)
        pulse = math.sin(math.pi * (index + 0.5) / steps)
        stress = stress.at[2, 0].add(pulse * load_map)
        history.append((state[3:], strain, plastic))
        state = jnp.concatenate([velocity, stress], 0)
    cotangent = end_cotangent
    totals = jnp.zeros((pulses,), jnp.float32)
    for index in reversed(range(steps)):
        pulse = math.sin(math.pi * (index + 0.5) / steps)
        surface = jnp.dot(onehot, cotangent[5, 0].reshape(-1), precision=lax.Precision.HIGHEST)
        totals = totals + pulse * surface * is_top
        old_stress, strain, plastic = history[index]
        _, pull = jax.vjp(
            lambda first, second, plastic=plastic: radial_return(
                first, second, lame, shear, yield_radius, plastic
            ),
            old_stress,
            strain,
        )
        stress_part, strain_cot = pull(cotangent[3:])
        velocity_cot, back = coupled(strain_cot, cotangent[:3], False, buoyancy)
        cotangent = jnp.concatenate([velocity_cot, stress_part - back], 0)
    summed = lax.psum(totals, ("depth", "lat"))
    scale = math.sqrt(pulses / (strip * lax.axis_size("lat") * across))
    return (cotangent, summed * scale)


def solution(mesh):
    placed = (
        P(None, "depth", "lat", None),
        P(None, "depth", "lat", None),
        P("depth", "lat", None),
        P(None, "depth", "lat", None),
        P("depth", "lat", None),
        P(None, "depth", "lat", None),
        P("lat", None),
        P(),
    )
    return jax.shard_map(
        per_device,
        mesh=mesh,
        in_specs=placed,
        out_specs=(P(None, "depth", "lat", None), P()),
        check_vma=False,
    )
```

profile of v0, /device:TPU:24, one launch (start us, length us, event | category | flops | bytes accessed | tf_op | source)
XLA Modules:
  0.0 359.3 jit_solution(10057530034631810376)
XLA Ops:
  14.5 5.2 %collective-permute-done.3 = f32[6,10,1,256]{3,2,1,0:T(1,128)S(1)} collective-permute-done((f32[6,10,1,256]{3,2,1,0:T(1,128)S(1)}, f32[6,10,1,256]{3,2,1,0:T(1,128)S(1)}, u32[]{:S(2)}, u32[]{:S(2)}) %collective-permute-start.3) | collective-permute-done | bytes 61472 | tf_op jit(solution)/shard_map/ppermute | solution.py:17
  31.1 3.9 %collective-permute-start.7 = (f32[3,10,1,256]{3,2,1,0:T(1,128)S(1)}, f32[3,10,1,256]{3,2,1,0:T(1,128)S(1)}, u32[]{:S(2)}, u32[]{:S(2)}) collective-permute-start(f32[3,10,1,256]{3,2,1,0:T(1,128)S(1)} %get-tuple-element.215), channel_id=1, source_target_pairs={{1,0},{2,1},{3,2},{4,3},{5,4},{6,5},{7,6},{8,7},{9,8},{10,9},{11,1... | collective-permute-start | bytes 92168 | tf_op jit(solution)/shard_map/ppermute | solution.py:17
  50.9 3.9 %collective-permute-start.11 = (f32[6,10,1,256]{3,2,1,0:T(1,128)S(1)}, f32[6,10,1,256]{3,2,1,0:T(1,128)S(1)}, u32[]{:S(2)}, u32[]{:S(2)}) collective-permute-start(f32[6,10,1,256]{3,2,1,0:T(1,128)S(1)} %get-tuple-element.161), channel_id=1, source_target_pairs={{1,0},{2,1},{3,2},{4,3},{5,4},{6,5},{7,6},{8,7},{9,8},{10,9},{11,1... | collective-permute-start | bytes 184328 | tf_op jit(solution)/shard_map/ppermute | solution.py:17
  55.1 4.0 %collective-permute-done.11 = f32[6,10,1,256]{3,2,1,0:T(1,128)S(1)} collective-permute-done((f32[6,10,1,256]{3,2,1,0:T(1,128)S(1)}, f32[6,10,1,256]{3,2,1,0:T(1,128)S(1)}, u32[]{:S(2)}, u32[]{:S(2)}) %collective-permute-start.11) | collective-permute-done | bytes 61472 | tf_op jit(solution)/shard_map/ppermute | solution.py:17
  60.0 4.0 %collective-permute-start.12 = (f32[3,1,16,256]{3,2,1,0:T(8,128)S(1)}, f32[3,1,16,256]{3,2,1,0:T(8,128)S(1)}, u32[]{:S(2)}, u32[]{:S(2)}) collective-permute-start(f32[3,1,16,256]{3,2,1,0:T(8,128)S(1)} %get-tuple-element.226), channel_id=1, source_target_pairs={{0,16},{16,32},{32,48},{48,64},{64,80},{80,96},{96,112},{112,128},... | collective-permute-start | bytes 147464 | tf_op jit(solution)/shard_map/ppermute | solution.py:14
  69.7 3.9 %collective-permute-start.15 = (f32[3,10,1,256]{3,2,1,0:T(1,128)S(1)}, f32[3,10,1,256]{3,2,1,0:T(1,128)S(1)}, u32[]{:S(2)}, u32[]{:S(2)}) collective-permute-start(f32[3,10,1,256]{3,2,1,0:T(1,128)S(1)} %get-tuple-element.213), channel_id=1, source_target_pairs={{1,0},{2,1},{3,2},{4,3},{5,4},{6,5},{7,6},{8,7},{9,8},{10,9},{11,1... | collective-permute-start | bytes 92168 | tf_op jit(solution)/shard_map/ppermute | solution.py:17
  73.6 4.0 %collective-permute-done.15 = f32[3,10,1,256]{3,2,1,0:T(1,128)S(1)} collective-permute-done((f32[3,10,1,256]{3,2,1,0:T(1,128)S(1)}, f32[3,10,1,256]{3,2,1,0:T(1,128)S(1)}, u32[]{:S(2)}, u32[]{:S(2)}) %collective-permute-start.15) | collective-permute-done | bytes 30752 | tf_op jit(solution)/shard_map/ppermute | solution.py:17
  88.3 3.9 %collective-permute-start.19 = (f32[6,10,1,256]{3,2,1,0:T(1,128)S(1)}, f32[6,10,1,256]{3,2,1,0:T(1,128)S(1)}, u32[]{:S(2)}, u32[]{:S(2)}) collective-permute-start(f32[6,10,1,256]{3,2,1,0:T(1,128)S(1)} %get-tuple-element.159), channel_id=1, source_target_pairs={{1,0},{2,1},{3,2},{4,3},{5,4},{6,5},{7,6},{8,7},{9,8},{10,9},{11,1... | collective-permute-start | bytes 184328 | tf_op jit(solution)/shard_map/ppermute | solution.py:17
  92.5 4.0 %collective-permute-done.19 = f32[6,10,1,256]{3,2,1,0:T(1,128)S(1)} collective-permute-done((f32[6,10,1,256]{3,2,1,0:T(1,128)S(1)}, f32[6,10,1,256]{3,2,1,0:T(1,128)S(1)}, u32[]{:S(2)}, u32[]{:S(2)}) %collective-permute-start.19) | collective-permute-done | bytes 61472 | tf_op jit(solution)/shard_map/ppermute | solution.py:17
  97.4 5.4 %collective-permute-start.20 = (f32[3,1,16,256]{3,2,1,0:T(8,128)S(1)}, f32[3,1,16,256]{3,2,1,0:T(8,128)S(1)}, u32[]{:S(2)}, u32[]{:S(2)}) collective-permute-start(f32[3,1,16,256]{3,2,1,0:T(8,128)S(1)} %get-tuple-element.224), channel_id=1, source_target_pairs={{0,16},{16,32},{32,48},{48,64},{64,80},{80,96},{96,112},{112,128},... | collective-permute-start | bytes 147464 | tf_op jit(solution)/shard_map/ppermute | solution.py:14
  112.4 4.0 %collective-permute-done.23 = f32[3,10,1,256]{3,2,1,0:T(1,128)S(1)} collective-permute-done((f32[3,10,1,256]{3,2,1,0:T(1,128)S(1)}, f32[3,10,1,256]{3,2,1,0:T(1,128)S(1)}, u32[]{:S(2)}, u32[]{:S(2)}) %collective-permute-start.23) | collective-permute-done | bytes 30752 | tf_op jit(solution)/shard_map/ppermute | solution.py:17
  118.7 4.8 %collective-permute-start.24 = (f32[6,1,16,256]{3,2,1,0:T(8,128)S(1)}, f32[6,1,16,256]{3,2,1,0:T(8,128)S(1)}, u32[]{:S(2)}, u32[]{:S(2)}) collective-permute-start(f32[6,1,16,256]{3,2,1,0:T(8,128)S(1)} %get-tuple-element.168), channel_id=1, source_target_pairs={{0,16},{16,32},{32,48},{48,64},{64,80},{80,96},{96,112},{112,128},... | collective-permute-start | bytes 294920 | tf_op jit(solution)/shard_map/ppermute | solution.py:14
  133.6 4.0 %collective-permute-done.27 = f32[6,10,1,256]{3,2,1,0:T(1,128)S(1)} collective-permute-done((f32[6,10,1,256]{3,2,1,0:T(1,128)S(1)}, f32[6,10,1,256]{3,2,1,0:T(1,128)S(1)}, u32[]{:S(2)}, u32[]{:S(2)}) %collective-permute-start.27) | collective-permute-done | bytes 61472 | tf_op jit(solution)/shard_map/ppermute | solution.py:17
  138.5 5.1 %collective-permute-start.28 = (f32[3,1,16,256]{3,2,1,0:T(8,128)S(1)}, f32[3,1,16,256]{3,2,1,0:T(8,128)S(1)}, u32[]{:S(2)}, u32[]{:S(2)}) collective-permute-start(f32[3,1,16,256]{3,2,1,0:T(8,128)S(1)} %get-tuple-element.220), channel_id=1, source_target_pairs={{0,16},{16,32},{32,48},{48,64},{64,80},{80,96},{96,112},{112,128},... | collective-permute-start | bytes 147464 | tf_op jit(solution)/shard_map/ppermute | solution.py:14
  153.2 4.0 %collective-permute-done.31 = f32[3,10,1,256]{3,2,1,0:T(1,128)S(1)} collective-permute-done((f32[3,10,1,256]{3,2,1,0:T(1,128)S(1)}, f32[3,10,1,256]{3,2,1,0:T(1,128)S(1)}, u32[]{:S(2)}, u32[]{:S(2)}) %collective-permute-start.31) | collective-permute-done | bytes 30752 | tf_op jit(solution)/shard_map/ppermute | solution.py:17
  160.1 4.8 %collective-permute-start.32 = (f32[6,1,16,256]{3,2,1,0:T(8,128)S(1)}, f32[6,1,16,256]{3,2,1,0:T(8,128)S(1)}, u32[]{:S(2)}, u32[]{:S(2)}) collective-permute-start(f32[6,1,16,256]{3,2,1,0:T(8,128)S(1)} %get-tuple-element.166), channel_id=1, source_target_pairs={{0,16},{16,32},{32,48},{48,64},{64,80},{80,96},{96,112},{112,128},... | collective-permute-start | bytes 294920 | tf_op jit(solution)/shard_map/ppermute | solution.py:14
  171.4 4.1 %collective-permute-start.35 = (f32[6,10,1,256]{3,2,1,0:T(1,128)}, f32[6,10,1,256]{3,2,1,0:T(1,128)}, u32[]{:S(2)}, u32[]{:S(2)}) collective-permute-start(f32[6,10,1,256]{3,2,1,0:T(1,128)} %get-tuple-element.155), channel_id=1, source_target_pairs={{1,0},{2,1},{3,2},{4,3},{5,4},{6,5},{7,6},{8,7},{9,8},{10,9},{11,1... | collective-permute-start | bytes 184328 | tf_op jit(solution)/shard_map/ppermute | solution.py:17
  182.5 5.1 %collective-permute-start.36 = (f32[3,1,16,256]{3,2,1,0:T(8,128)S(1)}, f32[3,1,16,256]{3,2,1,0:T(8,128)S(1)}, u32[]{:S(2)}, u32[]{:S(2)}) collective-permute-start(f32[3,1,16,256]{3,2,1,0:T(8,128)S(1)} %get-tuple-element.218), channel_id=1, source_target_pairs={{0,16},{16,32},{32,48},{48,64},{64,80},{80,96},{96,112},{112,128},... | collective-permute-start | bytes 147464 | tf_op jit(solution)/shard_map/ppermute | solution.py:14
  205.3 4.8 %collective-permute-start.40 = (f32[6,1,16,256]{3,2,1,0:T(8,128)S(1)}, f32[6,1,16,256]{3,2,1,0:T(8,128)S(1)}, u32[]{:S(2)}, u32[]{:S(2)}) collective-permute-start(f32[6,1,16,256]{3,2,1,0:T(8,128)S(1)} %get-tuple-element.164), channel_id=1, source_target_pairs={{0,16},{16,32},{32,48},{48,64},{64,80},{80,96},{96,112},{112,128},... | collective-permute-start | bytes 294920 | tf_op jit(solution)/shard_map/ppermute | solution.py:14
  216.0 3.9 %collective-permute-start.43 = (f32[6,10,1,256]{3,2,1,0:T(1,128)S(1)}, f32[6,10,1,256]{3,2,1,0:T(1,128)S(1)}, u32[]{:S(2)}, u32[]{:S(2)}) collective-permute-start(f32[6,10,1,256]{3,2,1,0:T(1,128)S(1)} %get-tuple-element.153), channel_id=1, source_target_pairs={{1,0},{2,1},{3,2},{4,3},{5,4},{6,5},{7,6},{8,7},{9,8},{10,9},{11,1... | collective-permute-start | bytes 184328 | tf_op jit(solution)/shard_map/ppermute | solution.py:17
  220.2 4.0 %collective-permute-done.43 = f32[6,10,1,256]{3,2,1,0:T(1,128)S(1)} collective-permute-done((f32[6,10,1,256]{3,2,1,0:T(1,128)S(1)}, f32[6,10,1,256]{3,2,1,0:T(1,128)S(1)}, u32[]{:S(2)}, u32[]{:S(2)}) %collective-permute-start.43) | collective-permute-done | bytes 61472 | tf_op jit(solution)/shard_map/ppermute | solution.py:17
  225.2 5.1 %collective-permute-start.44 = (f32[3,1,16,256]{3,2,1,0:T(8,128)S(1)}, f32[3,1,16,256]{3,2,1,0:T(8,128)S(1)}, u32[]{:S(2)}, u32[]{:S(2)}) collective-permute-start(f32[3,1,16,256]{3,2,1,0:T(8,128)S(1)} %get-tuple-element.216), channel_id=1, source_target_pairs={{0,16},{16,32},{32,48},{48,64},{64,80},{80,96},{96,112},{112,128},... | collective-permute-start | bytes 147464 | tf_op jit(solution)/shard_map/ppermute | solution.py:14
  232.1 113.2 %psum.7 = f32[64]{0:T(128)S(1)} all-reduce(f32[64]{0:T(128)S(1)} %fusion.1), channel_id=1, replica_groups=mesh['depth'=32,'lat'=16] {'depth','lat'}, use_global_device_ids=true, to_apply=%region_0.0 | all-reduce | flops 64 | bytes 512 | tf_op jit(solution)/shard_map/psum | solution.py:151
  351.8 4.9 %collective-permute-done.47 = f32[3,10,1,256]{3,2,1,0:T(1,128)S(1)} collective-permute-done((f32[3,10,1,256]{3,2,1,0:T(1,128)S(1)}, f32[3,10,1,256]{3,2,1,0:T(1,128)S(1)}, u32[]{:S(2)}, u32[]{:S(2)}) %collective-permute-start.47) | collective-permute-done | bytes 30752 | tf_op jit(solution)/shard_map/ppermute | solution.py:17
  (309 shorter events, 142.7 us)
Async XLA Ops:
  8.4 6.1 %collective-permute-start.2 = (f32[6,10,1,256]{3,2,1,0:T(1,128)S(1)}, f32[6,10,1,256]{3,2,1,0:T(1,128)S(1)}, u32[]{:S(2)}, u32[]{:S(2)}) collective-permute-start(f32[6,10,1,256]{3,2,1,0:T(1,128)S(1)} %get-tuple-element.162), channel_id=1, source_target_pairs={{0,1},{1,2},{2,3},{3,4},{4,5},{5,6},{6,7},{7,8},{8,9},{9,10},{10,1... | collective-permute-start | bytes 184328 | tf_op jit(solution)/shard_map/ppermute | solution.py:14
  11.4 8.2 %collective-permute-start.3 = (f32[6,10,1,256]{3,2,1,0:T(1,128)S(1)}, f32[6,10,1,256]{3,2,1,0:T(1,128)S(1)}, u32[]{:S(2)}, u32[]{:S(2)}) collective-permute-start(f32[6,10,1,256]{3,2,1,0:T(1,128)S(1)} %get-tuple-element.163), channel_id=1, source_target_pairs={{1,0},{2,1},{3,2},{4,3},{5,4},{6,5},{7,6},{8,7},{9,8},{10,9},{11,1... | collective-permute-start | bytes 184328 | tf_op jit(solution)/shard_map/ppermute | solution.py:17
  31.1 7.9 %collective-permute-start.7 = (f32[3,10,1,256]{3,2,1,0:T(1,128)S(1)}, f32[3,10,1,256]{3,2,1,0:T(1,128)S(1)}, u32[]{:S(2)}, u32[]{:S(2)}) collective-permute-start(f32[3,10,1,256]{3,2,1,0:T(1,128)S(1)} %get-tuple-element.215), channel_id=1, source_target_pairs={{1,0},{2,1},{3,2},{4,3},{5,4},{6,5},{7,6},{8,7},{9,8},{10,9},{11,1... | collective-permute-start | bytes 92168 | tf_op jit(solution)/shard_map/ppermute | solution.py:17
  49.0 6.1 %collective-permute-start.10 = (f32[6,10,1,256]{3,2,1,0:T(1,128)S(1)}, f32[6,10,1,256]{3,2,1,0:T(1,128)S(1)}, u32[]{:S(2)}, u32[]{:S(2)}) collective-permute-start(f32[6,10,1,256]{3,2,1,0:T(1,128)S(1)} %get-tuple-element.160), channel_id=1, source_target_pairs={{0,1},{1,2},{2,3},{3,4},{4,5},{5,6},{6,7},{7,8},{8,9},{9,10},{10,1... | collective-permute-start | bytes 184328 | tf_op jit(solution)/shard_map/ppermute | solution.py:14
  50.9 8.2 %collective-permute-start.11 = (f32[6,10,1,256]{3,2,1,0:T(1,128)S(1)}, f32[6,10,1,256]{3,2,1,0:T(1,128)S(1)}, u32[]{:S(2)}, u32[]{:S(2)}) collective-permute-start(f32[6,10,1,256]{3,2,1,0:T(1,128)S(1)} %get-tuple-element.161), channel_id=1, source_target_pairs={{1,0},{2,1},{3,2},{4,3},{5,4},{6,5},{7,6},{8,7},{9,8},{10,9},{11,1... | collective-permute-start | bytes 184328 | tf_op jit(solution)/shard_map/ppermute | solution.py:17
  69.7 7.9 %collective-permute-start.15 = (f32[3,10,1,256]{3,2,1,0:T(1,128)S(1)}, f32[3,10,1,256]{3,2,1,0:T(1,128)S(1)}, u32[]{:S(2)}, u32[]{:S(2)}) collective-permute-start(f32[3,10,1,256]{3,2,1,0:T(1,128)S(1)} %get-tuple-element.213), channel_id=1, source_target_pairs={{1,0},{2,1},{3,2},{4,3},{5,4},{6,5},{7,6},{8,7},{9,8},{10,9},{11,1... | collective-permute-start | bytes 92168 | tf_op jit(solution)/shard_map/ppermute | solution.py:17
  88.3 8.2 %collective-permute-start.19 = (f32[6,10,1,256]{3,2,1,0:T(1,128)S(1)}, f32[6,10,1,256]{3,2,1,0:T(1,128)S(1)}, u32[]{:S(2)}, u32[]{:S(2)}) collective-permute-start(f32[6,10,1,256]{3,2,1,0:T(1,128)S(1)} %get-tuple-element.159), channel_id=1, source_target_pairs={{1,0},{2,1},{3,2},{4,3},{5,4},{6,5},{7,6},{8,7},{9,8},{10,9},{11,1... | collective-permute-start | bytes 184328 | tf_op jit(solution)/shard_map/ppermute | solution.py:17
  97.4 6.7 %collective-permute-start.20 = (f32[3,1,16,256]{3,2,1,0:T(8,128)S(1)}, f32[3,1,16,256]{3,2,1,0:T(8,128)S(1)}, u32[]{:S(2)}, u32[]{:S(2)}) collective-permute-start(f32[3,1,16,256]{3,2,1,0:T(8,128)S(1)} %get-tuple-element.224), channel_id=1, source_target_pairs={{0,16},{16,32},{32,48},{48,64},{64,80},{80,96},{96,112},{112,128},... | collective-permute-start | bytes 147464 | tf_op jit(solution)/shard_map/ppermute | solution.py:14
  108.5 7.9 %collective-permute-start.23 = (f32[3,10,1,256]{3,2,1,0:T(1,128)S(1)}, f32[3,10,1,256]{3,2,1,0:T(1,128)S(1)}, u32[]{:S(2)}, u32[]{:S(2)}) collective-permute-start(f32[3,10,1,256]{3,2,1,0:T(1,128)S(1)} %get-tuple-element.211), channel_id=1, source_target_pairs={{1,0},{2,1},{3,2},{4,3},{5,4},{6,5},{7,6},{8,7},{9,8},{10,9},{11,1... | collective-permute-start | bytes 92168 | tf_op jit(solution)/shard_map/ppermute | solution.py:17
  118.7 6.1 %collective-permute-start.24 = (f32[6,1,16,256]{3,2,1,0:T(8,128)S(1)}, f32[6,1,16,256]{3,2,1,0:T(8,128)S(1)}, u32[]{:S(2)}, u32[]{:S(2)}) collective-permute-start(f32[6,1,16,256]{3,2,1,0:T(8,128)S(1)} %get-tuple-element.168), channel_id=1, source_target_pairs={{0,16},{16,32},{32,48},{48,64},{64,80},{80,96},{96,112},{112,128},... | collective-permute-start | bytes 294920 | tf_op jit(solution)/shard_map/ppermute | solution.py:14
  129.4 8.2 %collective-permute-start.27 = (f32[6,10,1,256]{3,2,1,0:T(1,128)S(1)}, f32[6,10,1,256]{3,2,1,0:T(1,128)S(1)}, u32[]{:S(2)}, u32[]{:S(2)}) collective-permute-start(f32[6,10,1,256]{3,2,1,0:T(1,128)S(1)} %get-tuple-element.157), channel_id=1, source_target_pairs={{1,0},{2,1},{3,2},{4,3},{5,4},{6,5},{7,6},{8,7},{9,8},{10,9},{11,1... | collective-permute-start | bytes 184328 | tf_op jit(solution)/shard_map/ppermute | solution.py:17
  138.5 6.4 %collective-permute-start.28 = (f32[3,1,16,256]{3,2,1,0:T(8,128)S(1)}, f32[3,1,16,256]{3,2,1,0:T(8,128)S(1)}, u32[]{:S(2)}, u32[]{:S(2)}) collective-permute-start(f32[3,1,16,256]{3,2,1,0:T(8,128)S(1)} %get-tuple-element.220), channel_id=1, source_target_pairs={{0,16},{16,32},{32,48},{48,64},{64,80},{80,96},{96,112},{112,128},... | collective-permute-start | bytes 147464 | tf_op jit(solution)/shard_map/ppermute | solution.py:14
  149.3 7.9 %collective-permute-start.31 = (f32[3,10,1,256]{3,2,1,0:T(1,128)S(1)}, f32[3,10,1,256]{3,2,1,0:T(1,128)S(1)}, u32[]{:S(2)}, u32[]{:S(2)}) collective-permute-start(f32[3,10,1,256]{3,2,1,0:T(1,128)S(1)} %get-tuple-element.209), channel_id=1, source_target_pairs={{1,0},{2,1},{3,2},{4,3},{5,4},{6,5},{7,6},{8,7},{9,8},{10,9},{11,1... | collective-permute-start | bytes 92168 | tf_op jit(solution)/shard_map/ppermute | solution.py:17
  160.1 6.1 %collective-permute-start.32 = (f32[6,1,16,256]{3,2,1,0:T(8,128)S(1)}, f32[6,1,16,256]{3,2,1,0:T(8,128)S(1)}, u32[]{:S(2)}, u32[]{:S(2)}) collective-permute-start(f32[6,1,16,256]{3,2,1,0:T(8,128)S(1)} %get-tuple-element.166), channel_id=1, source_target_pairs={{0,16},{16,32},{32,48},{48,64},{64,80},{80,96},{96,112},{112,128},... | collective-permute-start | bytes 294920 | tf_op jit(solution)/shard_map/ppermute | solution.py:14
  169.5 6.7 %collective-permute-start.34 = (f32[6,10,1,256]{3,2,1,0:T(1,128)}, f32[6,10,1,256]{3,2,1,0:T(1,128)}, u32[]{:S(2)}, u32[]{:S(2)}) collective-permute-start(f32[6,10,1,256]{3,2,1,0:T(1,128)} %get-tuple-element.154), channel_id=1, source_target_pairs={{0,1},{1,2},{2,3},{3,4},{4,5},{5,6},{6,7},{7,8},{8,9},{9,10},{10,1... | collective-permute-start | bytes 184328 | tf_op jit(solution)/shard_map/ppermute | solution.py:14
  171.4 8.5 %collective-permute-start.35 = (f32[6,10,1,256]{3,2,1,0:T(1,128)}, f32[6,10,1,256]{3,2,1,0:T(1,128)}, u32[]{:S(2)}, u32[]{:S(2)}) collective-permute-start(f32[6,10,1,256]{3,2,1,0:T(1,128)} %get-tuple-element.155), channel_id=1, source_target_pairs={{1,0},{2,1},{3,2},{4,3},{5,4},{6,5},{7,6},{8,7},{9,8},{10,9},{11,1... | collective-permute-start | bytes 184328 | tf_op jit(solution)/shard_map/ppermute | solution.py:17
  182.5 7.0 %collective-permute-start.36 = (f32[3,1,16,256]{3,2,1,0:T(8,128)S(1)}, f32[3,1,16,256]{3,2,1,0:T(8,128)S(1)}, u32[]{:S(2)}, u32[]{:S(2)}) collective-permute-start(f32[3,1,16,256]{3,2,1,0:T(8,128)S(1)} %get-tuple-element.218), channel_id=1, source_target_pairs={{0,16},{16,32},{32,48},{48,64},{64,80},{80,96},{96,112},{112,128},... | collective-permute-start | bytes 147464 | tf_op jit(solution)/shard_map/ppermute | solution.py:14
  193.2 7.9 %collective-permute-start.39 = (f32[3,10,1,256]{3,2,1,0:T(1,128)S(1)}, f32[3,10,1,256]{3,2,1,0:T(1,128)S(1)}, u32[]{:S(2)}, u32[]{:S(2)}) collective-permute-start(f32[3,10,1,256]{3,2,1,0:T(1,128)S(1)} %get-tuple-element.207), channel_id=1, source_target_pairs={{1,0},{2,1},{3,2},{4,3},{5,4},{6,5},{7,6},{8,7},{9,8},{10,9},{11,1... | collective-permute-start | bytes 92168 | tf_op jit(solution)/shard_map/ppermute | solution.py:17
  205.3 6.7 %collective-permute-start.40 = (f32[6,1,16,256]{3,2,1,0:T(8,128)S(1)}, f32[6,1,16,256]{3,2,1,0:T(8,128)S(1)}, u32[]{:S(2)}, u32[]{:S(2)}) collective-permute-start(f32[6,1,16,256]{3,2,1,0:T(8,128)S(1)} %get-tuple-element.164), channel_id=1, source_target_pairs={{0,16},{16,32},{32,48},{48,64},{64,80},{80,96},{96,112},{112,128},... | collective-permute-start | bytes 294920 | tf_op jit(solution)/shard_map/ppermute | solution.py:14
  216.0 8.2 %collective-permute-start.43 = (f32[6,10,1,256]{3,2,1,0:T(1,128)S(1)}, f32[6,10,1,256]{3,2,1,0:T(1,128)S(1)}, u32[]{:S(2)}, u32[]{:S(2)}) collective-permute-start(f32[6,10,1,256]{3,2,1,0:T(1,128)S(1)} %get-tuple-element.153), channel_id=1, source_target_pairs={{1,0},{2,1},{3,2},{4,3},{5,4},{6,5},{7,6},{8,7},{9,8},{10,9},{11,1... | collective-permute-start | bytes 184328 | tf_op jit(solution)/shard_map/ppermute | solution.py:17
  225.2 120.2 %collective-permute-start.44 = (f32[3,1,16,256]{3,2,1,0:T(8,128)S(1)}, f32[3,1,16,256]{3,2,1,0:T(8,128)S(1)}, u32[]{:S(2)}, u32[]{:S(2)}) collective-permute-start(f32[3,1,16,256]{3,2,1,0:T(8,128)S(1)} %get-tuple-element.216), channel_id=1, source_target_pairs={{0,16},{16,32},{32,48},{48,64},{64,80},{80,96},{96,112},{112,128},... | collective-permute-start | bytes 147464 | tf_op jit(solution)/shard_map/ppermute | solution.py:14
  230.3 115.1 %collective-permute-start.45 = (f32[3,1,16,256]{3,2,1,0:T(8,128)S(1)}, f32[3,1,16,256]{3,2,1,0:T(8,128)S(1)}, u32[]{:S(2)}, u32[]{:S(2)}) collective-permute-start(f32[3,1,16,256]{3,2,1,0:T(8,128)S(1)} %get-tuple-element.217), channel_id=1, source_target_pairs={{16,0},{32,16},{48,32},{64,48},{80,64},{96,80},{112,96},{128,112},... | collective-permute-start | bytes 147464 | tf_op jit(solution)/shard_map/ppermute | solution.py:17
  345.4 6.4 %collective-permute-start.46 = (f32[3,10,1,256]{3,2,1,0:T(1,128)S(1)}, f32[3,10,1,256]{3,2,1,0:T(1,128)S(1)}, u32[]{:S(2)}, u32[]{:S(2)}) collective-permute-start(f32[3,10,1,256]{3,2,1,0:T(1,128)S(1)} %get-tuple-element.204), channel_id=1, source_target_pairs={{0,1},{1,2},{2,3},{3,4},{4,5},{5,6},{6,7},{7,8},{8,9},{9,10},{10,1... | collective-permute-start | bytes 92168 | tf_op jit(solution)/shard_map/ppermute | solution.py:14
  348.8 7.9 %collective-permute-start.47 = (f32[3,10,1,256]{3,2,1,0:T(1,128)S(1)}, f32[3,10,1,256]{3,2,1,0:T(1,128)S(1)}, u32[]{:S(2)}, u32[]{:S(2)}) collective-permute-start(f32[3,10,1,256]{3,2,1,0:T(1,128)S(1)} %get-tuple-element.205), channel_id=1, source_target_pairs={{1,0},{2,1},{3,2},{4,3},{5,4},{6,5},{7,6},{8,7},{9,8},{10,9},{11,1... | collective-permute-start | bytes 92168 | tf_op jit(solution)/shard_map/ppermute | solution.py:17
  (61 other events, 288.6 us)
where the time goes:
time: 361 us; the launch traced here: 359 us
  starting transfers between devices  137 us (38%)
  blocking collectives  113 us (31%)
  waiting for transfers between devices  76.8 us (21%)
  other arithmetic  16.6 us (5%)
  local copies, waits for them, and re-layouts  10.6 us (3%)
    psum x1, blocking collectives, per_device(): summed = lax.psum(totals, ('depth', 'lat'))  113 us
    ppermute x24, starting transfers between devices, with_halo(): lax.ppermute(lax.slice_in_dim(block, block.shape[dim] - width, None, axis...  77.3 us
    ppermute x24, waiting for transfers between devices, with_halo(): lax.ppermute(lax.slice_in_dim(block, 0, width, axis=dim), axis, backward)  75.6 us
    ppermute x24, starting transfers between devices, with_halo(): lax.ppermute(lax.slice_in_dim(block, 0, width, axis=dim), axis, backward)  60.2 us
  transfers between devices with their start and end apart: 48, of which 28 were waited for; matrix products, arithmetic and copies ran while one was open for 1% of the time, Pallas kernels for 0%

commit v1 on v0

v1 whole, which is shorter than its diff:
```python
import functools
import math

import jax
import jax.numpy as jnp
from jax import lax
from jax.experimental import pallas as pl
from jax.experimental.pallas import tpu as pltpu
from jax.sharding import PartitionSpec as P

MESH = pl.DeviceIdType.MESH
F32 = jnp.float32

NZ_OWN = 8
NX_OWN = 16
GROUP = 24
LAYER = 2 * GROUP
BASE = 8
ROWS = BASE + (NZ_OWN + 4) * LAYER


def row_of(z, x, half=0):
    return BASE + LAYER * (z + 2) + GROUP * half + x


class Tile:
    def __init__(self, row, stride=1):
        self.row = row
        self.stride = stride

    def at(self, half, shift=0):
        start = self.row + GROUP * half + shift
        return pl.ds(start, 8) if self.stride == 1 else pl.ds(start, 8, self.stride)

    def load(self, ref, field, dz=0, dx=0):
        return [ref[field, self.at(half, LAYER * dz + dx), :] for half in range(2)]

    def store(self, ref, field, half, value):
        ref[field, self.at(half), :] = value


def y_shifts():
    lane = lax.broadcasted_iota(jnp.int32, (8, 128), 1)
    first = lane == 0
    last = lane == 127

    def before(pair):
        low, high = pltpu.roll(pair[0], 1, 1), pltpu.roll(pair[1], 1, 1)
        return [jnp.where(first, 0.0, low), jnp.where(first, low, high)]

    def after(pair):
        low, high = pltpu.roll(pair[0], 127, 1), pltpu.roll(pair[1], 127, 1)
        return [jnp.where(last, high, low), jnp.where(last, 0.0, high)]

    return before, after


def divergence(tile, ref):
    before, after = y_shifts()
    c = [tile.load(ref, k) for k in range(6)]
    xx_next = tile.load(ref, 0, dx=1)
    xy_prev = tile.load(ref, 3, dx=-1)
    xz_prev = tile.load(ref, 4, dx=-1)
    xz_up = tile.load(ref, 4, dz=-1)
    yz_up = tile.load(ref, 5, dz=-1)
    zz_down = tile.load(ref, 2, dz=1)
    xy_y = before(c[3])
    yz_y = before(c[5])
    yy_y = after(c[1])
    out = []
    for h in range(2):
        out.append(
            (
                (xx_next[h] - c[0][h]) + (c[3][h] - xy_y[h]) + (c[4][h] - xz_up[h]),
                (c[3][h] - xy_prev[h]) + (yy_y[h] - c[1][h]) + (c[5][h] - yz_up[h]),
                (c[4][h] - xz_prev[h]) + (c[5][h] - yz_y[h]) + (zz_down[h] - c[2][h]),
            )
        )
    return out


def gradient(tile, ref):
    before, after = y_shifts()
    w = [tile.load(ref, k) for k in range(3)]
    wx_prev = tile.load(ref, 0, dx=-1)
    wz_up = tile.load(ref, 2, dz=-1)
    wy_next = tile.load(ref, 1, dx=1)
    wz_next = tile.load(ref, 2, dx=1)
    wx_down = tile.load(ref, 0, dz=1)
    wy_down = tile.load(ref, 1, dz=1)
    wy_y = before(w[1])
    wx_y = after(w[0])
    wz_y = after(w[2])
    out = []
    for h in range(2):
        out.append(
            (
                w[0][h] - wx_prev[h],
                w[1][h] - wy_y[h],
                w[2][h] - wz_up[h],
                (wx_y[h] - w[0][h]) + (wy_next[h] - w[1][h]),
                (wx_down[h] - w[0][h]) + (wz_next[h] - w[2][h]),
                (wy_down[h] - w[1][h]) + (wz_y[h] - w[2][h]),
            )
        )
    return out


def trial(s, e, lame, shear, limit, plastic):
    volume = lame * (e[0] + e[1] + e[2])
    twice = 2.0 * shear
    normal = [s[a] + volume + twice * e[a] for a in range(3)]
    shears = [s[a] + shear * e[a] for a in range(3, 6)]
    mean = (normal[0] + normal[1] + normal[2]) * (1.0 / 3.0)
    devs = [normal[a] - mean for a in range(3)]
    qsq = (devs[0] * devs[0] + devs[1] * devs[1] + devs[2] * devs[2]) + 2.0 * (
        shears[0] * shears[0] + shears[1] * shears[1] + shears[2] * shears[2]
    )
    inverse = lax.rsqrt(limit * limit + qsq)
    scaled = plastic * limit * inverse
    factor = (1.0 - plastic) + scaled
    slope = scaled * (inverse * inverse)
    return mean, devs + shears, factor, slope


def pull_back(g, parts, factor, slope, lame, shear):
    along = (g[0] * parts[0] + g[1] * parts[1] + g[2] * parts[2]) + (
        g[3] * parts[3] + g[4] * parts[4] + g[5] * parts[5]
    )
    pull = slope * along
    pull_twice = pull + pull
    total = g[0] + g[1] + g[2]
    rest = (1.0 - factor) * (total * (1.0 / 3.0))
    twice = 2.0 * shear
    volume = lame * total
    stress = [factor * g[a] - pull * parts[a] + rest for a in range(3)]
    stress += [factor * g[a] - pull_twice * parts[a] for a in range(3, 6)]
    strain = [volume + twice * stress[a] for a in range(3)]
    strain += [shear * stress[a] for a in range(3, 6)]
    return stress, strain


TO_LOW = (0, 1, 2, 3, 4, 5)
TO_HIGH = (3, 4, 0, 1, 2, 5)
WIDE_LOW = ((0, 0, 16), (1, 0, 16), (2, 0, 16), (1, 1, 17), (2, 1, 17))
WIDE_HIGH = ((0, 15, -1), (1, 15, -1), (2, 15, -1), (0, 14, -2))
THIN_LOW = ((1, 0, 16), (2, 0, 16))
THIN_HIGH = ((0, 15, -1),)


def kernel(
    nd, nl, steps, pulses, wide_y,
    cp_in, ec_in, bu_in, mo_in, yi_in, ma_in, fp_ref, amp_ref,
    out_ref, pulse_ref,
    cp, ec, bu, mo, yi, ma,
    st, sp, co, vs, vb, hist, cf,
    load_map, q_map, fx_send, fx_low, fx_high, zs_low, zs_high, zc_low, zc_high, zm_low, zm_high,
    vx_send, vx_low, vx_high, cor_send, cor_recv,
    psum_buf, ysum_buf, xsum_buf, total_buf,
    in_sem, send_sem, recv_sem, far_sem,
):
    d = lax.axis_index("depth")
    l = lax.axis_index("lat")
    top = d == 0
    bottom = d == nd - 1
    has_low = l > 0
    has_high = l < nl - 1
    up = lax.rem(d + nd - 1, nd)
    down = lax.rem(d + 1, nd)
    low = jnp.maximum(l - 1, 0)
    high = jnp.minimum(l + 1, nl - 1)
    gains = [math.sin(math.pi * (n + 0.5) / steps) for n in range(steps)]

    loads = []
    for k, (source, target) in enumerate(((cp_in, cp), (mo_in, mo), (yi_in, yi), (ma_in, ma), (bu_in, bu), (ec_in, ec))):
        copy = pltpu.make_async_copy(source, target, in_sem.at[k])
        copy.start()
        loads.append(copy)

    barrier = pltpu.get_barrier_semaphore()

    def greet(dd, ll):
        pl.semaphore_signal(barrier, inc=1, device_id=(dd, ll), device_id_type=MESH)

    greet(up, l)
    greet(down, l)

    @pl.when(has_low)
    def _():
        greet(d, low)
        greet(up, low)
        greet(down, low)

    @pl.when(has_high)
    def _():
        greet(d, high)
        greet(up, high)
        greet(down, high)

    l_y = lax.rem(l, wide_y)
    l_x = l // wide_y
    n_x = nl // wide_y
    y_peers = [l_x * wide_y + lax.rem(l_y + k, wide_y) for k in range(1, wide_y)]
    x_peers = [lax.rem(l_x + k, n_x) * wide_y + l_y for k in range(1, n_x)]

    @pl.when(top)
    def _():
        for peer in y_peers + x_peers:
            greet(d, peer)

    ids = iter(range(1000))

    def remote(source, target, where):
        k = next(ids)
        return pltpu.make_async_remote_copy(
            src_ref=source, dst_ref=target, send_sem=send_sem.at[k], recv_sem=recv_sem.at[k],
            device_id=where, device_id_type=MESH,
        )

    def own(z, t, h):
        return (z, pl.ds(8 * t, 8), pl.ds(128 * h, 128))

    def stage(z, carry):
        for t in range(2):
            for h in range(2):
                place = pl.ds(row_of(z, 8 * t, h), 8)
                for k in range(6):
                    st[k, place, :] = cp[(3 + k,) + own(z, t, h)]
                cf[0, place, :] = mo[(0,) + own(z, t, h)]
                cf[1, place, :] = mo[(1,) + own(z, t, h)]
                cf[2, place, :] = yi[own(z, t, h)]
                for k in range(3):
                    cf[3 + k, place, :] = ma[(k,) + own(z, t, h)].astype(F32)
        return carry

    def stage_end(z, carry):
        for t in range(2):
            for h in range(2):
                place = pl.ds(row_of(z, 8 * t, h), 8)
                for k in range(6):
                    sp[k, place, :] = ec[(3 + k,) + own(z, t, h)]
        return carry

    for copy in loads[:4]:
        copy.wait()
    lax.fori_loop(0, NZ_OWN, stage, 0)

    load_map[...] = jnp.zeros_like(load_map)

    @pl.when(top)
    def _():
        for t in range(2):
            for h in range(2):
                foot = fp_ref[pl.ds(8 * t, 8), pl.ds(128 * h, 128)]

                def add(p, total, foot=foot):
                    return jnp.where(foot == p, amp_ref[p], total)

                load_map[pl.ds(BASE + GROUP * h + 8 * t, 8), :] = lax.fori_loop(
                    0, pulses, add, jnp.zeros((8, 128), F32), unroll=8
                )

    zero = jnp.zeros((8, 128), F32)

    @pl.when(jnp.logical_not(has_low))
    def _():
        fx_low[...] = jnp.zeros_like(fx_low)
        vx_low[...] = jnp.zeros_like(vx_low)
        for p in range(2 * steps - 1):
            cor_recv[p, 0] = zero
            cor_recv[p, 1] = zero

    @pl.when(jnp.logical_not(has_high))
    def _():
        fx_high[...] = jnp.zeros_like(fx_high)
        vx_high[...] = jnp.zeros_like(vx_high)
        for p in range(2 * steps - 1):
            cor_recv[p, 2] = zero
            cor_recv[p, 3] = zero

    def face(ref, field, x, h):
        return ref[field, pl.ds(row_of(0, x, h), NZ_OWN, LAYER), :]

    for side, order, x in ((0, TO_LOW, 0), (1, TO_HIGH, NX_OWN - 1)):
        for k, field in enumerate(order):
            for h in range(2):
                fx_send[side, 2 * k + h] = face(st, field, x, h)
        for k in range(6):
            for h in range(2):
                fx_send[side, 12 + 2 * k + h] = face(cf, k, x, h)
        for h in range(2):
            fx_send[side, 24, pl.ds(h, 1), :] = load_map[pl.ds(BASE + GROUP * h + x, 1), :]

    near = 2 + 3 * has_low.astype(jnp.int32) + 3 * has_high.astype(jnp.int32)
    pl.semaphore_wait(barrier, near + top.astype(jnp.int32) * (len(y_peers) + len(x_peers)))

    class Exchange:
        def __init__(self):
            self.depth, self.low, self.high = [], [], []

        def start(self):
            for copy in self.depth:
                copy.start()

            @pl.when(has_low)
            def _():
                for copy in self.low:
                    copy.start()

            @pl.when(has_high)
            def _():
                for copy in self.high:
                    copy.start()

        def wait_send(self):
            for copy in self.depth:
                copy.wait_send()

            @pl.when(has_low)
            def _():
                for copy in self.low:
                    copy.wait_send()

            @pl.when(has_high)
            def _():
                for copy in self.high:
                    copy.wait_send()

        def wait_recv(self):
            for copy in self.depth:
                copy.wait_recv()

            @pl.when(has_high)
            def _():
                for copy in self.low:
                    copy.wait_recv()

            @pl.when(has_low)
            def _():
                for copy in self.high:
                    copy.wait_recv()

    last = NZ_OWN - 1
    first_faces = Exchange()
    first_faces.depth = [
        remote(cp.at[pl.ds(7, 2), last], zs_low.at[pl.ds(4, 2)], (down, l)),
        remote(cp.at[pl.ds(5, 1), 0], zs_high.at[pl.ds(2, 1)], (up, l)),
    ]
    first_faces.low = [remote(fx_send.at[0, pl.ds(0, 2)], fx_high.at[pl.ds(0, 2)], (d, low))]
    first_faces.high = [remote(fx_send.at[1, pl.ds(0, 4)], fx_low.at[pl.ds(0, 4)], (d, high))]
    first_faces.start()
    rest = Exchange()
    rest.depth = [
        remote(cp.at[pl.ds(3, 4), last], zs_low.at[pl.ds(0, 4)], (down, l)),
        remote(mo.at[:, last], zc_low.at[pl.ds(0, 2)], (down, l)),
        remote(yi.at[pl.ds(last, 1)], zc_low.at[pl.ds(2, 1)], (down, l)),
        remote(ma.at[:, last], zm_low, (down, l)),
        remote(cp.at[pl.ds(3, 2), 0], zs_high.at[pl.ds(0, 2)], (up, l)),
        remote(cp.at[pl.ds(6, 3), 0], zs_high.at[pl.ds(3, 3)], (up, l)),
        remote(mo.at[:, 0], zc_high.at[pl.ds(0, 2)], (up, l)),
        remote(yi.at[pl.ds(0, 1)], zc_high.at[pl.ds(2, 1)], (up, l)),
        remote(ma.at[:, 0], zm_high, (up, l)),
    ]
    rest.low = [remote(fx_send.at[0, pl.ds(2, 23)], fx_high.at[pl.ds(2, 23)], (d, low))]
    rest.high = [remote(fx_send.at[1, pl.ds(4, 21)], fx_low.at[pl.ds(4, 21)], (d, high))]
    rest.start()

    for copy in loads[4:]:
        copy.wait()
    lax.fori_loop(0, NZ_OWN, stage_end, 0)
    for side, x in ((0, 0), (1, NX_OWN - 1)):
        for k in range(6):
            for h in range(2):
                fx_send[side, 25 + 2 * k + h] = face(sp, k, x, h)
    ends = Exchange()
    ends.depth = [
        remote(ec.at[pl.ds(3, 6), last], zs_low.at[pl.ds(6, 6)], (down, l)),
        remote(ec.at[pl.ds(3, 6), 0], zs_high.at[pl.ds(6, 6)], (up, l)),
    ]
    ends.low = [remote(fx_send.at[0, pl.ds(25, 12)], fx_high.at[pl.ds(25, 12)], (d, low))]
    ends.high = [remote(fx_send.at[1, pl.ds(25, 12)], fx_low.at[pl.ds(25, 12)], (d, high))]
    ends.start()

    def put_face(ref, field, x, h, value):
        ref[field, pl.ds(row_of(0, x, h), NZ_OWN, LAYER), :] = value

    def put_layer(ref, field, z, source, outside):
        for t in range(2):
            for h in range(2):
                value = source[pl.ds(8 * t, 8), pl.ds(128 * h, 128)].astype(F32)
                if outside is not None:
                    value = jnp.where(outside, 0.0, value)
                ref[field, pl.ds(row_of(z, 8 * t, h), 8), :] = value

    def put_stress(fields):
        for field in fields[0]:
            put_layer(st, field, -1, zs_low.at[field], top)
        for field in fields[1]:
            put_layer(st, field, NZ_OWN, zs_high.at[field], bottom)
        for field in fields[2]:
            for h in range(2):
                put_face(st, field, -1, h, fx_low[2 * TO_HIGH.index(field) + h])
        for field in fields[3]:
            for h in range(2):
                put_face(st, field, NX_OWN, h, fx_high[2 * TO_LOW.index(field) + h])

    inside_z = [jnp.logical_not(top), jnp.logical_not(bottom)]

    def everywhere(unit):
        def inner(z, carry):
            for t in range(2):
                unit(Tile(row_of(z, 8 * t)), None)
            return carry

        lax.fori_loop(0, NZ_OWN, inner, 0)

        def outer(i, carry):
            side = i // 2
            z = -1 + (NZ_OWN + 1) * side
            inside = jnp.where(side == 0, inside_z[0].astype(jnp.int32), inside_z[1].astype(jnp.int32)) > 0
            unit(Tile(row_of(z, 8 * lax.rem(i, 2))), inside)
            return carry

        lax.fori_loop(0, 4, outer, 0)
        unit(Tile(row_of(0, -1), LAYER), has_low)
        unit(Tile(row_of(0, NX_OWN), LAYER), has_high)

    def keep(inside, value):
        return value if inside is None else jnp.where(inside, value, 0.0)

    def coefficients(tile, n):
        return [tile.load(cf, k) for k in (0, 1, 2, 3 + n)]

    def forward_stress(n):
        v = vs.at[n]
        record = hist.at[n]

        def unit(tile, inside):
            e = gradient(tile, v)
            s = [tile.load(st, k) for k in range(6)]
            lame, shear, limit, plastic = coefficients(tile, n)
            for h in range(2):
                mean, parts, factor, slope = trial(
                    [s[k][h] for k in range(6)], e[h], lame[h], shear[h], limit[h], plastic[h]
                )
                for k in range(6):
                    value = factor * parts[k]
                    if k < 3:
                        value = mean + value
                    tile.store(st, k, h, keep(inside, value))
                    tile.store(record, k, h, parts[k])
                tile.store(record, 6, h, factor)
                tile.store(record, 7, h, slope)

        everywhere(unit)

        @pl.when(top)
        def _():
            for h in range(2):
                for x, count in ((-1, 1), (0, 8), (8, 8), (16, 1)):
                    place = pl.ds(row_of(0, x, h), count)
                    st[2, place, :] += gains[n] * load_map[pl.ds(BASE + GROUP * h + x, count), :]

    def turn():
        n = steps - 1
        v = vs.at[n]

        def unit(tile, inside):
            e = gradient(tile, v)
            s = [tile.load(st, k) for k in range(6)]
            g = [tile.load(sp, k) for k in range(6)]
            lame, shear, limit, plastic = coefficients(tile, n)
            for h in range(2):
                mean, parts, factor, slope = trial(
                    [s[k][h] for k in range(6)], e[h], lame[h], shear[h], limit[h], plastic[h]
                )
                stress, strain = pull_back([g[k][h] for k in range(6)], parts, factor, slope, lame[h], shear[h])
                for k in range(6):
                    tile.store(sp, k, h, stress[k])
                    tile.store(co, k, h, keep(inside, strain[k]))

        everywhere(unit)

    def backward_stress(n):
        w = vs.at[2 * steps - 2 - n]
        record = hist.at[n]

        def unit(tile, inside):
            back = gradient(tile, w)
            s = [tile.load(sp, k) for k in range(6)]
            kept = [tile.load(record, k) for k in range(8)]
            lame, shear = tile.load(cf, 0), tile.load(cf, 1)
            for h in range(2):
                g = [s[k][h] - back[h][k] for k in range(6)]
                stress, strain = pull_back(
                    g, [kept[k][h] for k in range(6)], kept[6][h], kept[7][h], lame[h], shear[h]
                )
                for k in range(6):
                    tile.store(sp, k, h, stress[k])
                    tile.store(co, k, h, keep(inside, strain[k]))

        everywhere(unit)

    def forward_velocity(n):
        def body(z, carry):
            for t in range(2):
                tile = Tile(row_of(z, 8 * t))
                div = divergence(tile, st)
                for h in range(2):
                    b = bu[own(z, t, h)]
                    for k in range(3):
                        old = cp[(k,) + own(z, t, h)] if n == 0 else vs[n - 1, k, tile.at(h), :]
                        vs[n, k, tile.at(h), :] = old + b * div[h][k]
            return carry

        lax.fori_loop(0, NZ_OWN, body, 0)

    def backward_velocity(n):
        slot = 2 * steps - 1 - n

        def body(z, carry):
            for t in range(2):
                tile = Tile(row_of(z, 8 * t))
                div = divergence(tile, co)
                for h in range(2):
                    b = bu[own(z, t, h)]
                    for k in range(3):
                        source = ec if n == steps - 1 else vb
                        new = source[(k,) + own(z, t, h)] - div[h][k]
                        target = vb if n > 0 else out_ref
                        target[(k,) + own(z, t, h)] = new
                        vs[slot, k, tile.at(h), :] = b * new
            return carry

        lax.fori_loop(0, NZ_OWN, body, 0)

    corner_fields = ((0, 2), (0, 1), (1, 2), (0, 1, 2))

    def send_velocity(p):
        v = vs.at[p]
        wide = p < 2 * steps - 1
        to_low, to_high = (WIDE_LOW, WIDE_HIGH) if wide else (THIN_LOW, THIN_HIGH)
        step = Exchange()

        def layers(field, count, z, depth):
            return v.at[pl.ds(field, count), pl.ds(row_of(z, 0), depth * LAYER), :]

        if wide:
            step.depth = [
                remote(layers(0, 2, last, 1), layers(0, 2, -1, 1), (down, l)),
                remote(layers(2, 1, last - 1, 2), layers(2, 1, -2, 2), (down, l)),
                remote(layers(0, 2, 0, 2), layers(0, 2, NZ_OWN, 2), (up, l)),
                remote(layers(2, 1, 0, 1), layers(2, 1, NZ_OWN, 1), (up, l)),
            ]
        else:
            step.depth = [
                remote(layers(2, 1, last, 1), layers(2, 1, -1, 1), (down, l)),
                remote(layers(0, 2, 0, 1), layers(0, 2, NZ_OWN, 1), (up, l)),
            ]
        for k, (field, here, there) in enumerate(to_low):
            for h in range(2):
                vx_send[p, 0, 2 * k + h] = face(v, field, here, h)
        for k, (field, here, there) in enumerate(to_high):
            for h in range(2):
                vx_send[p, 1, 2 * k + h] = face(v, field, here, h)
        if wide:
            for c, (x, z) in enumerate(((15, last), (15, 0), (0, last), (0, 0))):
                for field in corner_fields[c]:
                    for h in range(2):
                        cor_send[p, c, pl.ds(2 * field + h, 1), :] = v[field, pl.ds(row_of(z, x, h), 1), :]
            step.high = [
                remote(cor_send.at[p, 0], cor_recv.at[p, 0], (down, high)),
                remote(cor_send.at[p, 1], cor_recv.at[p, 1], (up, high)),
            ]
            step.low = [
                remote(cor_send.at[p, 2], cor_recv.at[p, 2], (down, low)),
                remote(cor_send.at[p, 3], cor_recv.at[p, 3], (up, low)),
            ]
        count = 2 * len(to_low)
        step.low.append(remote(vx_send.at[p, 0, pl.ds(0, count)], vx_high.at[p, pl.ds(0, count)], (d, low)))
        count = 2 * len(to_high)
        step.high.append(remote(vx_send.at[p, 1, pl.ds(0, count)], vx_low.at[p, pl.ds(0, count)], (d, high)))
        step.start()
        return step

    def take_velocity(p, step):
        v = vs.at[p]
        wide = p < 2 * steps - 1
        to_low, to_high = (WIDE_LOW, WIDE_HIGH) if wide else (THIN_LOW, THIN_HIGH)
        step.wait_send()
        step.wait_recv()

        def clear(field, z, depth):
            def body(i, carry):
                v[field, pl.ds(row_of(z, 0) + 8 * i, 8), :] = zero
                return carry

            lax.fori_loop(0, depth * LAYER // 8, body, 0)

        @pl.when(top)
        def _():
            if wide:
                clear(0, -1, 1)
                clear(1, -1, 1)
                clear(2, -2, 2)
            else:
                clear(2, -1, 1)

        @pl.when(bottom)
        def _():
            for field in range(2):
                clear(field, NZ_OWN, 2 if wide else 1)
            if wide:
                clear(2, NZ_OWN, 1)

        for k, (field, here, there) in enumerate(to_low):
            for h in range(2):
                put_face(v, field, there, h, vx_high[p, 2 * k + h])
        for k, (field, here, there) in enumerate(to_high):
            for h in range(2):
                put_face(v, field, there, h, vx_low[p, 2 * k + h])
        if wide:
            for c, (x, z, outside) in enumerate(
                ((-1, -1, top), (-1, NZ_OWN, bottom), (NX_OWN, -1, top), (NX_OWN, NZ_OWN, bottom))
            ):
                for field in corner_fields[c]:
                    for h in range(2):
                        value = cor_recv[p, c, pl.ds(2 * field + h, 1), :]
                        v[field, pl.ds(row_of(z, x, h), 1), :] = jnp.where(outside, 0.0, value)

    rounds = []
    reach = 2
    while reach < nd // 2:
        rounds.append(reach)
        reach *= 2

    def far_signal(i):
        if i < len(rounds):
            for way, other in enumerate((lax.rem(d + rounds[i], nd), lax.rem(d + nd - rounds[i], nd))):
                pl.semaphore_signal(far_sem.at[2 * i + way], inc=1, device_id=(other, l), device_id_type=MESH)

    def far_wait(i):
        if i < len(rounds):
            for way in range(2):
                pl.semaphore_wait(far_sem.at[2 * i + way], 1)

    def note_surface(gain, w_slot, start):
        @pl.when(top)
        def _():
            for t in range(2):
                for h in range(2):
                    place = pl.ds(row_of(0, 8 * t, h), 8)
                    if w_slot is None:
                        value = sp[2, place, :]
                    else:
                        value = sp[2, place, :] - vs[w_slot, 2, place, :]
                    spot = pl.ds(16 * h + 8 * t, 8)
                    q_map[spot, :] = gain * value if start else q_map[spot, :] + gain * value

    y_copies = [remote(psum_buf.at[0], ysum_buf.at[l_y], (d, peer)) for peer in y_peers]
    x_copies = [remote(psum_buf.at[1], xsum_buf.at[l_x], (d, peer)) for peer in x_peers]

    def add_up_pulses():
        @pl.when(top)
        def _():
            bins = lax.broadcasted_iota(jnp.int32, (pulses, 128), 0)
            total = jnp.zeros((pulses, 128), F32)
            for t in range(2):
                for h in range(2):
                    foot = fp_ref[pl.ds(8 * t, 8), pl.ds(128 * h, 128)]
                    value = q_map[pl.ds(16 * h + 8 * t, 8), :]
                    for i in range(8):
                        total = total + jnp.where(
                            jnp.broadcast_to(foot[i : i + 1], (pulses, 128)) == bins,
                            jnp.broadcast_to(value[i : i + 1], (pulses, 128)),
                            0.0,
                        )
            sums = lax.dot_general(
                jnp.ones((8, 128), F32), total, (((1,), (1,)), ((), ())),
                precision=lax.Precision.HIGHEST, preferred_element_type=F32,
            )
            psum_buf[0] = zero
            psum_buf[0, :, pl.ds(0, pulses)] = sums
            for copy in y_copies:
                copy.start()
            ysum_buf[l_y] = psum_buf[0]
            for copy in y_copies:
                copy.wait_recv()
            sums = ysum_buf[0]
            for k in range(1, wide_y):
                sums = sums + ysum_buf[k]
            psum_buf[1] = sums
            for copy in x_copies:
                copy.start()
            xsum_buf[l_x] = sums
            for copy in y_copies:
                copy.wait_send()

    chips = nd // 2
    far = sorted(range(1, chips), key=lambda k: -min(k, chips - k))
    far_ids = [next(ids) for _ in far]
    core_id = next(ids)

    def spread_copy(k, send_id):
        return pltpu.make_async_remote_copy(
            src_ref=total_buf, dst_ref=total_buf, send_sem=send_sem.at[send_id], recv_sem=recv_sem.at[far_ids[0]],
            device_id=(2 * k, l), device_id_type=MESH,
        )

    core_copy = pltpu.make_async_remote_copy(
        src_ref=total_buf, dst_ref=total_buf, send_sem=send_sem.at[core_id], recv_sem=recv_sem.at[core_id],
        device_id=(d + 1 - 2 * lax.rem(d, 2), l), device_id_type=MESH,
    )
    scale = math.sqrt(pulses / (NX_OWN * nl * 256))

    def spread_pulses():
        @pl.when(top)
        def _():
            for copy in x_copies:
                copy.wait_recv()
            sums = xsum_buf[0]
            for k in range(1, n_x):
                sums = sums + xsum_buf[k]
            total_buf[...] = sums * scale
            for k, send_id in zip(far, far_ids):
                spread_copy(k, send_id).start()
            core_copy.start()
            for copy in x_copies:
                copy.wait_send()

    def finish_pulses():
        even = lax.rem(d, 2) == 0

        @pl.when(jnp.logical_and(even, jnp.logical_not(top)))
        def _():
            spread_copy(1, far_ids[0]).wait_recv()
            core_copy.start()

        @pl.when(jnp.logical_not(even))
        def _():
            core_copy.wait_recv()

        pulse_ref[...] = total_buf[...]

        @pl.when(even)
        def _():
            core_copy.wait_send()

        @pl.when(top)
        def _():
            for k, send_id in zip(far, far_ids):
                spread_copy(k, send_id).wait_send()

    note_surface(gains[steps - 1], None, True)
    first_faces.wait_recv()
    put_stress(((4, 5), (2,), (3, 4), (0,)))
    forward_velocity(0)
    step = send_velocity(0)
    far_signal(0)
    rest.wait_recv()
    put_stress(((0, 1, 2, 3), (0, 1, 3, 4, 5), (0, 1, 2, 5), (1, 2, 3, 4, 5)))
    for k in range(3):
        put_layer(cf, k, -1, zc_low.at[k], None)
        put_layer(cf, k, NZ_OWN, zc_high.at[k], None)
        put_layer(cf, 3 + k, -1, zm_low.at[k], None)
        put_layer(cf, 3 + k, NZ_OWN, zm_high.at[k], None)
    for k in range(6):
        for h in range(2):
            put_face(cf, k, -1, h, fx_low[12 + 2 * k + h])
            put_face(cf, k, NX_OWN, h, fx_high[12 + 2 * k + h])
    for h in range(2):
        load_map[pl.ds(BASE + GROUP * h - 1, 1), :] = fx_low[24, pl.ds(h, 1), :]
        load_map[pl.ds(BASE + GROUP * h + NX_OWN, 1), :] = fx_high[24, pl.ds(h, 1), :]
    for n in range(steps - 1):
        take_velocity(n, step)
        far_wait(n)
        forward_stress(n)
        forward_velocity(n + 1)
        step = send_velocity(n + 1)
        far_signal(n + 1)
        if n == 0:
            ends.wait_recv()
            for k in range(6):
                put_layer(sp, k, -1, zs_low.at[6 + k], None)
                put_layer(sp, k, NZ_OWN, zs_high.at[6 + k], None)
                for h in range(2):
                    put_face(sp, k, -1, h, fx_low[25 + 2 * k + h])
                    put_face(sp, k, NX_OWN, h, fx_high[25 + 2 * k + h])

    take_velocity(steps - 1, step)
    far_wait(steps - 1)
    turn()
    pulse_sends = []
    for n in range(steps - 1, -1, -1):
        backward_velocity(n)
        slot = 2 * steps - 1 - n
        step = send_velocity(slot)
        if n == 0:
            spread_pulses()
        if n > 0:
            note_surface(gains[n - 1], slot, False)
        if n == 1:
            add_up_pulses()
        take_velocity(slot, step)
        if n > 0:
            backward_stress(n - 1)

    def last_stress(z, carry):
        for t in range(2):
            tile = Tile(row_of(z, 8 * t))
            back = gradient(tile, vs.at[2 * steps - 1])
            for h in range(2):
                for k in range(6):
                    out_ref[(3 + k,) + own(z, t, h)] = sp[k, tile.at(h), :] - back[h][k]
        return carry

    lax.fori_loop(0, NZ_OWN, last_stress, 0)
    finish_pulses()
    for exchange in (first_faces, rest, ends):
        exchange.wait_send()


def per_device(mesh_shape, checkpoint, end_cotangent, buoyancy, moduli, yield_radius, mask, footprint, amplitude):
    steps = mask.shape[0]
    pulses = amplitude.shape[0]
    nd, nl = mesh_shape
    phases = 2 * steps
    vmem = pltpu.VMEM
    ext = (ROWS, 128)
    tile = (8, 128)
    anywhere = pl.BlockSpec(memory_space=pl.ANY)
    in_vmem = pl.BlockSpec(memory_space=pltpu.VMEM)
    scratch = [vmem(a.shape, a.dtype) for a in (checkpoint, end_cotangent, buoyancy, moduli, yield_radius, mask)]
    plane = checkpoint.shape[2:]
    scratch += [
        vmem((6,) + ext, F32),
        vmem((6,) + ext, F32),
        vmem((6,) + ext, F32),
        vmem((phases, 3) + ext, F32),
        vmem((3,) + buoyancy.shape, F32),
        vmem((steps - 1, 8) + ext, F32),
        vmem((3 + steps,) + ext, F32),
        vmem((64, 128), F32),
        vmem((32, 128), F32),
        vmem((2, 37) + tile, F32),
        vmem((37,) + tile, F32),
        vmem((37,) + tile, F32),
        vmem((12,) + plane, F32),
        vmem((12,) + plane, F32),
        vmem((3,) + plane, F32),
        vmem((3,) + plane, F32),
        vmem((steps,) + plane, jnp.int32),
        vmem((steps,) + plane, jnp.int32),
        vmem((phases, 2, 10) + tile, F32),
        vmem((phases, 10) + tile, F32),
        vmem((phases, 10) + tile, F32),
        vmem((phases - 1, 4) + tile, F32),
        vmem((phases - 1, 4) + tile, F32),
        vmem((2,) + tile, F32),
        vmem((4,) + tile, F32),
        vmem((4,) + tile, F32),
        vmem(tile, F32),
        pltpu.SemaphoreType.DMA((6,)),
        pltpu.SemaphoreType.DMA((112,)),
        pltpu.SemaphoreType.DMA((112,)),
        pltpu.SemaphoreType.REGULAR((8,)),
    ]
    adjoint, sums = pl.pallas_call(
        functools.partial(kernel, nd, nl, steps, pulses, 4),
        out_shape=(
            jax.ShapeDtypeStruct(checkpoint.shape, F32),
            jax.ShapeDtypeStruct(tile, F32),
        ),
        in_specs=[anywhere] * 6 + [in_vmem, pl.BlockSpec(memory_space=pltpu.SMEM)],
        out_specs=(in_vmem, in_vmem),
        scratch_shapes=scratch,
        compiler_params=pltpu.CompilerParams(
            collective_id=0, has_side_effects=True, vmem_limit_bytes=48 * 2**20
        ),
    )(checkpoint, end_cotangent, buoyancy, moduli, yield_radius, mask, footprint, amplitude)
    return adjoint, sums[0, :pulses]


def solution(mesh):
    placed = (
        P(None, "depth", "lat", None),
        P(None, "depth", "lat", None),
        P("depth", "lat", None),
        P(None, "depth", "lat", None),
        P("depth", "lat", None),
        P(None, "depth", "lat", None),
        P("lat", None),
        P(),
    )
    return jax.shard_map(
        functools.partial(per_device, (mesh.shape["depth"], mesh.shape["lat"])),
        mesh=mesh,
        in_specs=placed,
        out_specs=(P(None, "depth", "lat", None), P()),
        check_vma=False,
    )
```

time: 361 us -> 74.2 us (0.21)
  the two profiles are of different devices: /device:TPU:24 before, /device:TPU:33 now
where the time goes in v1:
time: 74.2 us; the launch traced here: 73.9 us
  Pallas kernels  64 us (86%)
  local copies, waits for them, and re-layouts  9.18 us (12%)
    pallas_call x1, Pallas kernels, per_device(): pl.pallas_call(functools.partial(kernel, nd, nl, steps, pulses, 4), out_s...  64 us
    unnamed x17, local copies, waits for them, and re-layouts  8.67 us

profile of v1, /device:TPU:33, one launch (start us, length us, event | category | flops | bytes accessed | tf_op | source)
XLA Modules:
  0.0 73.9 jit_solution(575488941624050259)
XLA Ops:
  0.6 0.0 copy-start
  0.6 1.3 %copy-done = f32[9,8,16,256]{3,2,1,0:T(8,128)S(1)} copy-done((f32[9,8,16,256]{3,2,1,0:T(8,128)S(1)}, f32[9,8,16,256]{3,2,1,0:T(8,128)}, u32[]{:S(2)}) %copy-start) | copy-done | bytes 1179672
  1.9 0.0 copy-start.1
  1.9 1.3 %copy-done.1 = f32[9,8,16,256]{3,2,1,0:T(8,128)S(1)} copy-done((f32[9,8,16,256]{3,2,1,0:T(8,128)S(1)}, f32[9,8,16,256]{3,2,1,0:T(8,128)}, u32[]{:S(2)}) %copy-start.1) | copy-done | bytes 1179672
  3.2 0.0 copy-start.2
  3.2 1.0 %copy-done.2 = s32[3,8,16,256]{3,2,1,0:T(8,128)S(1)} copy-done((s32[3,8,16,256]{3,2,1,0:T(8,128)S(1)}, s32[3,8,16,256]{3,2,1,0:T(8,128)}, u32[]{:S(2)}) %copy-start.2) | copy-done | bytes 393240
  4.2 0.0 copy-start.3
  4.2 0.9 %copy-done.3 = f32[2,8,16,256]{3,2,1,0:T(8,128)S(1)} copy-done((f32[2,8,16,256]{3,2,1,0:T(8,128)S(1)}, f32[2,8,16,256]{3,2,1,0:T(8,128)}, u32[]{:S(2)}) %copy-start.3) | copy-done | bytes 262168
  5.1 0.0 copy-start.4
  5.1 0.9 %copy-done.4 = f32[8,16,256]{2,1,0:T(8,128)S(1)} copy-done((f32[8,16,256]{2,1,0:T(8,128)S(1)}, f32[8,16,256]{2,1,0:T(8,128)}, u32[]{:S(2)}) %copy-start.4) | copy-done | bytes 131096
  6.0 0.0 copy-start.5
  6.0 0.9 %copy-done.5 = f32[8,16,256]{2,1,0:T(8,128)S(1)} copy-done((f32[8,16,256]{2,1,0:T(8,128)S(1)}, f32[8,16,256]{2,1,0:T(8,128)}, u32[]{:S(2)}) %copy-start.5) | copy-done | bytes 131096
  6.9 0.0 copy-start.6
  6.9 0.7 copy-done.6
  7.6 0.0 copy-start.7
  7.7 0.7 copy-done.7
  8.3 64.0 %shard_map.95 = (f32[9,8,16,256]{3,2,1,0:T(8,128)S(1)}, f32[8,128]{1,0:T(8,128)S(1)}) custom-call(f32[9,8,16,256]{3,2,1,0:T(8,128)S(1)} %copy-done, f32[9,8,16,256]{3,2,1,0:T(8,128)S(1)} %copy-done.1, f32[8,16,256]{2,1,0:T(8,128)S(1)} %copy-done.4, f32[2,8,16,256]{3,2,1,0:T(8,128)S(1)} %copy-done.3, f32[8,16,256]{2,1,0:T(8,128)S(1)} %copy-done.5, ...), custom_call_target="tpu_custom_call" | custom-call | tf_op jit(solution)/shard_map/pallas_call | solution.py:868
  72.3 0.5 slice_bitcast_fusion
  72.8 1.0 %copy.11 = f32[9,8,16,256]{3,2,1,0:T(8,128)} copy(f32[9,8,16,256]{3,2,1,0:T(8,128)S(1)} %get-tuple-element.8) | data formatting | bytes 2359296
Async XLA Ops:
  0.6 1.3 %copy-start = (f32[9,8,16,256]{3,2,1,0:T(8,128)S(1)}, f32[9,8,16,256]{3,2,1,0:T(8,128)}, u32[]{:S(2)}) copy-start(f32[9,8,16,256]{3,2,1,0:T(8,128)} %cp_in.1) | copy-start | bytes 3538948
  1.9 1.3 %copy-start.1 = (f32[9,8,16,256]{3,2,1,0:T(8,128)S(1)}, f32[9,8,16,256]{3,2,1,0:T(8,128)}, u32[]{:S(2)}) copy-start(f32[9,8,16,256]{3,2,1,0:T(8,128)} %ec_in.1) | copy-start | bytes 3538948
  3.2 1.0 %copy-start.2 = (s32[3,8,16,256]{3,2,1,0:T(8,128)S(1)}, s32[3,8,16,256]{3,2,1,0:T(8,128)}, u32[]{:S(2)}) copy-start(s32[3,8,16,256]{3,2,1,0:T(8,128)} %ma_in.1) | copy-start | bytes 1179652
  4.2 0.9 %copy-start.3 = (f32[2,8,16,256]{3,2,1,0:T(8,128)S(1)}, f32[2,8,16,256]{3,2,1,0:T(8,128)}, u32[]{:S(2)}) copy-start(f32[2,8,16,256]{3,2,1,0:T(8,128)} %mo_in.1) | copy-start | bytes 786436
  5.1 0.9 %copy-start.4 = (f32[8,16,256]{2,1,0:T(8,128)S(1)}, f32[8,16,256]{2,1,0:T(8,128)}, u32[]{:S(2)}) copy-start(f32[8,16,256]{2,1,0:T(8,128)} %bu_in.1) | copy-start | bytes 393220
  6.0 0.9 %copy-start.5 = (f32[8,16,256]{2,1,0:T(8,128)S(1)}, f32[8,16,256]{2,1,0:T(8,128)}, u32[]{:S(2)}) copy-start(f32[8,16,256]{2,1,0:T(8,128)} %yi_in.1) | copy-start | bytes 393220
  6.9 0.7 copy-start.6
  7.6 0.7 copy-start.7

commit v2 on v1

--- a/solution.py
+++ b/solution.py
@@ -16,6 +16,9 @@
 GROUP = 24
 LAYER = 2 * GROUP
 BASE = 8
+UNROLL_S = 2
+UNROLL_V = 8
+UNROLL_H = 2
 ROWS = BASE + (NZ_OWN + 4) * LAYER
 
 
@@ -35,8 +38,8 @@
     def load(self, ref, field, dz=0, dx=0):
         return [ref[field, self.at(half, LAYER * dz + dx), :] for half in range(2)]
 
-    def store(self, ref, field, half, value):
-        ref[field, self.at(half), :] = value
+    def store(self, later, ref, field, half, value):
+        later.append((ref, field, self.at(half), value))
 
 
 def y_shifts():
@@ -79,28 +82,35 @@
     return out
 
 
-def gradient(tile, ref):
+def y_differences(w):
     before, after = y_shifts()
+    wy_y, wx_y, wz_y = before(w[1]), after(w[0]), after(w[2])
+    return (
+        [w[1][h] - wy_y[h] for h in range(2)],
+        [wx_y[h] - w[0][h] for h in range(2)],
+        [wz_y[h] - w[2][h] for h in range(2)],
+    )
+
+
+def gradient(tile, ref, along_y=None):
     w = [tile.load(ref, k) for k in range(3)]
+    gy = y_differences(w) if along_y is None else [tile.load(along_y, k) for k in range(3)]
     wx_prev = tile.load(ref, 0, dx=-1)
     wz_up = tile.load(ref, 2, dz=-1)
     wy_next = tile.load(ref, 1, dx=1)
     wz_next = tile.load(ref, 2, dx=1)
     wx_down = tile.load(ref, 0, dz=1)
     wy_down = tile.load(ref, 1, dz=1)
-    wy_y = before(w[1])
-    wx_y = after(w[0])
-    wz_y = after(w[2])
     out = []
     for h in range(2):
         out.append(
             (
                 w[0][h] - wx_prev[h],
-                w[1][h] - wy_y[h],
+                gy[0][h],
                 w[2][h] - wz_up[h],
-                (wx_y[h] - w[0][h]) + (wy_next[h] - w[1][h]),
+                gy[1][h] + (wy_next[h] - w[1][h]),
                 (wx_down[h] - w[0][h]) + (wz_next[h] - w[2][h]),
-                (wy_down[h] - w[1][h]) + (wz_y[h] - w[2][h]),
+                (wy_down[h] - w[1][h]) + gy[2][h],
             )
         )
     return out
@@ -150,10 +160,10 @@
 
 def kernel(
     nd, nl, steps, pulses, wide_y,
-    cp_in, ec_in, bu_in, mo_in, yi_in, ma_in, fp_ref, amp_ref,
+    cp_in, ec_in, bu_in, mo_in, yi_in, ma_in, fp_in, amp_in,
     out_ref, pulse_ref,
-    cp, ec, bu, mo, yi, ma,
-    st, sp, co, vs, vb, hist, cf,
+    cp, ec, bu, mo, yi, ma, fp_ref, amp_ref,
+    st, sp, co, vs, vb, hist, cf, gy,
     load_map, q_map, fx_send, fx_low, fx_high, zs_low, zs_high, zc_low, zc_high, zm_low, zm_high,
     vx_send, vx_low, vx_high, cor_send, cor_recv,
     psum_buf, ysum_buf, xsum_buf, total_buf,
@@ -171,11 +181,12 @@
     high = jnp.minimum(l + 1, nl - 1)
     gains = [math.sin(math.pi * (n + 0.5) / steps) for n in range(steps)]
 
-    loads = []
-    for k, (source, target) in enumerate(((cp_in, cp), (mo_in, mo), (yi_in, yi), (ma_in, ma), (bu_in, bu), (ec_in, ec))):
+    def load_in(k, source, target):
         copy = pltpu.make_async_copy(source, target, in_sem.at[k])
         copy.start()
-        loads.append(copy)
+        return copy
+
+    stress_in = load_in(0, cp_in.at[pl.ds(3, 6)], cp.at[pl.ds(3, 6)])
 
     barrier = pltpu.get_barrier_semaphore()
 
@@ -208,6 +219,10 @@
         for peer in y_peers + x_peers:
             greet(d, peer)
 
+    others = ((mo_in, mo), (yi_in, yi), (ma_in, ma), (fp_in, fp_ref), (amp_in, amp_ref), (bu_in, bu), (ec_in, ec))
+    static_in = [load_in(1 + k, source, target) for k, (source, target) in enumerate(others[:5])]
+    velocity_in = load_in(6, cp_in.at[pl.ds(0, 3)], cp.at[pl.ds(0, 3)])
+    late_in = [load_in(7 + k, source, target) for k, (source, target) in enumerate(others[5:])]
     ids = iter(range(1000))
 
     def remote(source, target, where):
@@ -220,76 +235,22 @@
     def own(z, t, h):
         return (z, pl.ds(8 * t, 8), pl.ds(128 * h, 128))
 
-    def stage(z, carry):
+    def stage_stress(z, carry):
         for t in range(2):
             for h in range(2):
-                place = pl.ds(row_of(z, 8 * t, h), 8)
                 for k in range(6):
-                    st[k, place, :] = cp[(3 + k,) + own(z, t, h)]
-                cf[0, place, :] = mo[(0,) + own(z, t, h)]
-                cf[1, place, :] = mo[(1,) + own(z, t, h)]
-                cf[2, place, :] = yi[own(z, t, h)]
-                for k in range(3):
-                    cf[3 + k, place, :] = ma[(k,) + own(z, t, h)].astype(F32)
+                    st[k, pl.ds(row_of(z, 8 * t, h), 8), :] = cp[(3 + k,) + own(z, t, h)]
         return carry
-
-    def stage_end(z, carry):
-        for t in range(2):
-            for h in range(2):
-                place = pl.ds(row_of(z, 8 * t, h), 8)
-                for k in range(6):
-                    sp[k, place, :] = ec[(3 + k,) + own(z, t, h)]
-        return carry
-
-    for copy in loads[:4]:
-        copy.wait()
-    lax.fori_loop(0, NZ_OWN, stage, 0)
-
-    load_map[...] = jnp.zeros_like(load_map)
-
-    @pl.when(top)
-    def _():
-        for t in range(2):
-            for h in range(2):
-                foot = fp_ref[pl.ds(8 * t, 8), pl.ds(128 * h, 128)]
-
-                def add(p, total, foot=foot):
-                    return jnp.where(foot == p, amp_ref[p], total)
-
-                load_map[pl.ds(BASE + GROUP * h + 8 * t, 8), :] = lax.fori_loop(
-                    0, pulses, add, jnp.zeros((8, 128), F32), unroll=8
-                )
-
-    zero = jnp.zeros((8, 128), F32)
-
-    @pl.when(jnp.logical_not(has_low))
-    def _():
-        fx_low[...] = jnp.zeros_like(fx_low)
-        vx_low[...] = jnp.zeros_like(vx_low)
-        for p in range(2 * steps - 1):
-            cor_recv[p, 0] = zero
-            cor_recv[p, 1] = zero
-
-    @pl.when(jnp.logical_not(has_high))
-    def _():
-        fx_high[...] = jnp.zeros_like(fx_high)
-        vx_high[...] = jnp.zeros_like(vx_high)
-        for p in range(2 * steps - 1):
-            cor_recv[p, 2] = zero
-            cor_recv[p, 3] = zero
 
     def face(ref, field, x, h):
         return ref[field, pl.ds(row_of(0, x, h), NZ_OWN, LAYER), :]
 
-    for side, order, x in ((0, TO_LOW, 0), (1, TO_HIGH, NX_OWN - 1)):
-        for k, field in enumerate(order):
-            for h in range(2):
-                fx_send[side, 2 * k + h] = face(st, field, x, h)
-        for k in range(6):
-            for h in range(2):
-                fx_send[side, 12 + 2 * k + h] = face(cf, k, x, h)
-        for h in range(2):
-            fx_send[side, 24, pl.ds(h, 1), :] = load_map[pl.ds(BASE + GROUP * h + x, 1), :]
+    stress_in.wait()
+    lax.fori_loop(0, NZ_OWN, stage_stress, 0)
+    for side, order, x, count in ((0, TO_LOW, 0, 1), (1, TO_HIGH, NX_OWN - 1, 2)):
+        for k in range(count):
+            for h in range(2):
+                fx_send[side, 2 * k + h] = face(st, order[k], x, h)
 
     near = 2 + 3 * has_low.astype(jnp.int32) + 3 * has_high.astype(jnp.int32)
     pl.semaphore_wait(barrier, near + top.astype(jnp.int32) * (len(y_peers) + len(x_peers)))
@@ -299,9 +260,6 @@
             self.depth, self.low, self.high = [], [], []
 
         def start(self):
-            for copy in self.depth:
-                copy.start()
-
             @pl.when(has_low)
             def _():
                 for copy in self.low:
@@ -311,6 +269,9 @@
             def _():
                 for copy in self.high:
                     copy.start()
+
+            for copy in self.depth:
+                copy.start()
 
         def wait_send(self):
             for copy in self.depth:
@@ -349,6 +310,72 @@
     first_faces.low = [remote(fx_send.at[0, pl.ds(0, 2)], fx_high.at[pl.ds(0, 2)], (d, low))]
     first_faces.high = [remote(fx_send.at[1, pl.ds(0, 4)], fx_low.at[pl.ds(0, 4)], (d, high))]
     first_faces.start()
+    def stage(z, carry):
+        for t in range(2):
+            for h in range(2):
+                place = pl.ds(row_of(z, 8 * t, h), 8)
+                cf[0, place, :] = mo[(0,) + own(z, t, h)]
+                cf[1, place, :] = mo[(1,) + own(z, t, h)]
+                cf[2, place, :] = yi[own(z, t, h)]
+                for k in range(3):
+                    cf[3 + k, place, :] = ma[(k,) + own(z, t, h)].astype(F32)
+        return carry
+
+    def stage_end(z, carry):
+        for t in range(2):
+            for h in range(2):
+                place = pl.ds(row_of(z, 8 * t, h), 8)
+                for k in range(6):
+                    sp[k, place, :] = ec[(3 + k,) + own(z, t, h)]
+        return carry
+
+    for copy in static_in:
+        copy.wait()
+    lax.fori_loop(0, NZ_OWN, stage, 0)
+
+    load_map[...] = jnp.zeros_like(load_map)
+
+    @pl.when(top)
+    def _():
+        for t in range(2):
+            for h in range(2):
+                foot = fp_ref[pl.ds(8 * t, 8), pl.ds(128 * h, 128)]
+
+                def add(p, total, foot=foot):
+                    return jnp.where(foot == p, amp_ref[p], total)
+
+                load_map[pl.ds(BASE + GROUP * h + 8 * t, 8), :] = lax.fori_loop(
+                    0, pulses, add, jnp.zeros((8, 128), F32), unroll=8
+                )
+
+    zero = jnp.zeros((8, 128), F32)
+
+    @pl.when(jnp.logical_not(has_low))
+    def _():
+        fx_low[...] = jnp.zeros_like(fx_low)
+        vx_low[...] = jnp.zeros_like(vx_low)
+        for p in range(2 * steps - 1):
+            cor_recv[p, 0] = zero
+            cor_recv[p, 1] = zero
+
+    @pl.when(jnp.logical_not(has_high))
+    def _():
+        fx_high[...] = jnp.zeros_like(fx_high)
+        vx_high[...] = jnp.zeros_like(vx_high)
+        for p in range(2 * steps - 1):
+            cor_recv[p, 2] = zero
+            cor_recv[p, 3] = zero
+
+    for side, order, x, count in ((0, TO_LOW, 0, 1), (1, TO_HIGH, NX_OWN - 1, 2)):
+        for k in range(count, 6):
+            for h in range(2):
+                fx_send[side, 2 * k + h] = face(st, order[k], x, h)
+        for k in range(6):
+            for h in range(2):
+                fx_send[side, 12 + 2 * k + h] = face(cf, k, x, h)
+        for h in range(2):
+            fx_send[side, 24, pl.ds(h, 1), :] = load_map[pl.ds(BASE + GROUP * h + x, 1), :]
+
     rest = Exchange()
     rest.depth = [
         remote(cp.at[pl.ds(3, 4), last], zs_low.at[pl.ds(0, 4)], (down, l)),
@@ -365,7 +392,8 @@
     rest.high = [remote(fx_send.at[1, pl.ds(4, 21)], fx_low.at[pl.ds(4, 21)], (d, high))]
     rest.start()
 
-    for copy in loads[4:]:
+    velocity_in.wait()
+    for copy in late_in:
         copy.wait()
     lax.fori_loop(0, NZ_OWN, stage_end, 0)
     for side, x in ((0, 0), (1, NX_OWN - 1)):
@@ -406,24 +434,34 @@
 
     inside_z = [jnp.logical_not(top), jnp.logical_not(bottom)]
 
+    def write(later):
+        for ref, field, place, value in later:
+            ref[field, place, :] = value
+
     def everywhere(unit):
         def inner(z, carry):
+            later = []
             for t in range(2):
-                unit(Tile(row_of(z, 8 * t)), None)
+                unit(later, Tile(row_of(z, 8 * t)), None, gy)
+            write(later)
             return carry
 
-        lax.fori_loop(0, NZ_OWN, inner, 0)
-
-        def outer(i, carry):
-            side = i // 2
+        lax.fori_loop(0, NZ_OWN, inner, 0, unroll=UNROLL_S)
+
+        def outer(side, carry):
             z = -1 + (NZ_OWN + 1) * side
             inside = jnp.where(side == 0, inside_z[0].astype(jnp.int32), inside_z[1].astype(jnp.int32)) > 0
-            unit(Tile(row_of(z, 8 * lax.rem(i, 2))), inside)
+            later = []
+            for t in range(2):
+                unit(later, Tile(row_of(z, 8 * t)), inside, None)
+            write(later)
             return carry
 
-        lax.fori_loop(0, 4, outer, 0)
-        unit(Tile(row_of(0, -1), LAYER), has_low)
-        unit(Tile(row_of(0, NX_OWN), LAYER), has_high)
+        lax.fori_loop(0, 2, outer, 0, unroll=UNROLL_H)
+        later = []
+        unit(later, Tile(row_of(0, -1), LAYER), has_low, None)
+        unit(later, Tile(row_of(0, NX_OWN), LAYER), has_high, None)
+        write(later)
 
     def keep(inside, value):
         return value if inside is None else jnp.where(inside, value, 0.0)
@@ -435,8 +473,8 @@
         v = vs.at[n]
         record = hist.at[n]
 
-        def unit(tile, inside):
-            e = gradient(tile, v)
+        def unit(later, tile, inside, along_y):
+            e = gradient(tile, v, along_y)
             s = [tile.load(st, k) for k in range(6)]
             lame, shear, limit, plastic = coefficients(tile, n)
             for h in range(2):
@@ -447,10 +485,10 @@
                     value = factor * parts[k]
                     if k < 3:
                         value = mean + value
-                    tile.store(st, k, h, keep(inside, value))
-                    tile.store(record, k, h, parts[k])
-                tile.store(record, 6, h, factor)
-                tile.store(record, 7, h, slope)
+                    tile.store(later, st, k, h, keep(inside, value))
+                    tile.store(later, record, k, h, parts[k])
+                tile.store(later, record, 6, h, factor)
+                tile.store(later, record, 7, h, slope)
 
         everywhere(unit)
 
@@ -465,8 +503,8 @@
         n = steps - 1
         v = vs.at[n]
 
-        def unit(tile, inside):
-            e = gradient(tile, v)
+        def unit(later, tile, inside, along_y):
+            e = gradient(tile, v, along_y)
             s = [tile.load(st, k) for k in range(6)]
             g = [tile.load(sp, k) for k in range(6)]
             lame, shear, limit, plastic = coefficients(tile, n)
@@ -476,8 +514,8 @@
                 )
                 stress, strain = pull_back([g[k][h] for k in range(6)], parts, factor, slope, lame[h], shear[h])
                 for k in range(6):
-                    tile.store(sp, k, h, stress[k])
-                    tile.store(co, k, h, keep(inside, strain[k]))
+                    tile.store(later, sp, k, h, stress[k])
+                    tile.store(later, co, k, h, keep(inside, strain[k]))
 
         everywhere(unit)
 
@@ -485,8 +523,8 @@
         w = vs.at[2 * steps - 2 - n]
         record = hist.at[n]
 
-        def unit(tile, inside):
-            back = gradient(tile, w)
+        def unit(later, tile, inside, along_y):
+            back = gradient(tile, w, along_y)
             s = [tile.load(sp, k) for k in range(6)]
             kept = [tile.load(record, k) for k in range(8)]
             lame, shear = tile.load(cf, 0), tile.load(cf, 1)
@@ -496,13 +534,14 @@
                     g, [kept[k][h] for k in range(6)], kept[6][h], kept[7][h], lame[h], shear[h]
                 )
                 for k in range(6):
-                    tile.store(sp, k, h, stress[k])
-                    tile.store(co, k, h, keep(inside, strain[k]))
+                    tile.store(later, sp, k, h, stress[k])
+                    tile.store(later, co, k, h, keep(inside, strain[k]))
 
         everywhere(unit)
 
     def forward_velocity(n):
         def body(z, carry):
+            later = []
             for t in range(2):
                 tile = Tile(row_of(z, 8 * t))
                 div = divergence(tile, st)
@@ -510,15 +549,18 @@
                     b = bu[own(z, t, h)]
                     for k in range(3):
                         old = cp[(k,) + own(z, t, h)] if n == 0 else vs[n - 1, k, tile.at(h), :]
-                        vs[n, k, tile.at(h), :] = old + b * div[h][k]
+                        tile.store(later, vs.at[n], k, h, old + b * div[h][k])
+            write(later)
             return carry
 
-        lax.fori_loop(0, NZ_OWN, body, 0)
+        lax.fori_loop(0, NZ_OWN, body, 0, unroll=UNROLL_V)
 
     def backward_velocity(n):
         slot = 2 * steps - 1 - n
 
         def body(z, carry):
+            later = []
+            plain = []
             for t in range(2):
                 tile = Tile(row_of(z, 8 * t))
                 div = divergence(tile, co)
@@ -527,12 +569,15 @@
                     for k in range(3):
                         source = ec if n == steps - 1 else vb
                         new = source[(k,) + own(z, t, h)] - div[h][k]
-                        target = vb if n > 0 else out_ref
-                        target[(k,) + own(z, t, h)] = new
-                        vs[slot, k, tile.at(h), :] = b * new
+                        plain.append(((k,) + own(z, t, h), new))
+                        tile.store(later, vs.at[slot], k, h, b * new)
+            for place, new in plain:
+                target = vb if n > 0 else out_ref
+                target[place] = new
+            write(later)
             return carry
 
-        lax.fori_loop(0, NZ_OWN, body, 0)
+        lax.fori_loop(0, NZ_OWN, body, 0, unroll=UNROLL_V)
 
     corner_fields = ((0, 2), (0, 1), (1, 2), (0, 1, 2))
 
@@ -577,13 +622,30 @@
                 remote(cor_send.at[p, 3], cor_recv.at[p, 3], (up, low)),
             ]
         count = 2 * len(to_low)
-        step.low.append(remote(vx_send.at[p, 0, pl.ds(0, count)], vx_high.at[p, pl.ds(0, count)], (d, low)))
+        step.low.insert(0, remote(vx_send.at[p, 0, pl.ds(0, count)], vx_high.at[p, pl.ds(0, count)], (d, low)))
         count = 2 * len(to_high)
-        step.high.append(remote(vx_send.at[p, 1, pl.ds(0, count)], vx_low.at[p, pl.ds(0, count)], (d, high)))
+        step.high.insert(0, remote(vx_send.at[p, 1, pl.ds(0, count)], vx_low.at[p, pl.ds(0, count)], (d, high)))
         step.start()
         return step
 
+    def own_y_differences(p):
+        v = vs.at[p]
+
+        def body(z, carry):
+            later = []
+            for t in range(2):
+                tile = Tile(row_of(z, 8 * t))
+                parts = y_differences([tile.load(v, k) for k in range(3)])
+                for k in range(3):
+                    for h in range(2):
+                        tile.store(later, gy, k, h, parts[k][h])
+            write(later)
+            return carry
+
+        lax.fori_loop(0, NZ_OWN, body, 0, unroll=2)
+
     def take_velocity(p, step):
+        own_y_differences(p)
         v = vs.at[p]
         wide = p < 2 * steps - 1
         to_low, to_high = (WIDE_LOW, WIDE_HIGH) if wide else (THIN_LOW, THIN_HIGH)
@@ -740,7 +802,7 @@
         def _():
             core_copy.wait_recv()
 
-        pulse_ref[...] = total_buf[...]
+        pulse_ref[...] = total_buf[pl.ds(0, 1), pl.ds(0, pulses)]
 
         @pl.when(even)
         def _():
@@ -806,15 +868,18 @@
             backward_stress(n - 1)
 
     def last_stress(z, carry):
+        plain = []
         for t in range(2):
             tile = Tile(row_of(z, 8 * t))
-            back = gradient(tile, vs.at[2 * steps - 1])
+            back = gradient(tile, vs.at[2 * steps - 1], gy)
             for h in range(2):
                 for k in range(6):
-                    out_ref[(3 + k,) + own(z, t, h)] = sp[k, tile.at(h), :] - back[h][k]
+                    plain.append(((3 + k,) + own(z, t, h), sp[k, tile.at(h), :] - back[h][k]))
+        for place, value in plain:
+            out_ref[place] = value
         return carry
 
-    lax.fori_loop(0, NZ_OWN, last_stress, 0)
+    lax.fori_loop(0, NZ_OWN, last_stress, 0, unroll=UNROLL_S)
     finish_pulses()
     for exchange in (first_faces, rest, ends):
         exchange.wait_send()
@@ -828,9 +893,10 @@
     vmem = pltpu.VMEM
     ext = (ROWS, 128)
     tile = (8, 128)
-    anywhere = pl.BlockSpec(memory_space=pl.ANY)
+    in_hbm = pl.BlockSpec(memory_space=pltpu.HBM)
     in_vmem = pl.BlockSpec(memory_space=pltpu.VMEM)
     scratch = [vmem(a.shape, a.dtype) for a in (checkpoint, end_cotangent, buoyancy, moduli, yield_radius, mask)]
+    scratch += [vmem(footprint.shape, footprint.dtype), pltpu.SMEM(amplitude.shape, F32)]
     plane = checkpoint.shape[2:]
     scratch += [
         vmem((6,) + ext, F32),
@@ -840,6 +906,7 @@
         vmem((3,) + buoyancy.shape, F32),
         vmem((steps - 1, 8) + ext, F32),
         vmem((3 + steps,) + ext, F32),
+        vmem((3,) + ext, F32),
         vmem((64, 128), F32),
         vmem((32, 128), F32),
         vmem((2, 37) + tile, F32),
@@ -860,7 +927,7 @@
         vmem((4,) + tile, F32),
         vmem((4,) + tile, F32),
         vmem(tile, F32),
-        pltpu.SemaphoreType.DMA((6,)),
+        pltpu.SemaphoreType.DMA((9,)),
         pltpu.SemaphoreType.DMA((112,)),
         pltpu.SemaphoreType.DMA((112,)),
         pltpu.SemaphoreType.REGULAR((8,)),
@@ -868,17 +935,17 @@
     adjoint, sums = pl.pallas_call(
         functools.partial(kernel, nd, nl, steps, pulses, 4),
         out_shape=(
-            jax.ShapeDtypeStruct(checkpoint.shape, F32),
-            jax.ShapeDtypeStruct(tile, F32),
+            pltpu.VMEM(checkpoint.shape, F32),
+            pltpu.VMEM((1, pulses), F32),
         ),
-        in_specs=[anywhere] * 6 + [in_vmem, pl.BlockSpec(memory_space=pltpu.SMEM)],
+        in_specs=[in_hbm] * 8,
         out_specs=(in_vmem, in_vmem),
         scratch_shapes=scratch,
         compiler_params=pltpu.CompilerParams(
-            collective_id=0, has_side_effects=True, vmem_limit_bytes=48 * 2**20
+            collective_id=0, has_side_effects=True, vmem_limit_bytes=60 * 2**20
         ),
     )(checkpoint, end_cotangent, buoyancy, moduli, yield_radius, mask, footprint, amplitude)
-    return adjoint, sums[0, :pulses]
+    return adjoint, sums.reshape(pulses)
 
 
 def solution(mesh):

time: 74.2 us -> 53.7 us (0.72)
  Pallas kernels: 64 us -> 51.4 us
  local copies, waits for them, and re-layouts: 9.18 us -> 1.53 us
    pallas_call x1, Pallas kernels: 64 us -> 51.4 us  [per_device(): pl.pallas_call(functools.partial(kernel, nd, nl, steps, pulses, 4), out_s...]
    unnamed x17 -> x2, local copies, waits for them, and re-layouts: 8.67 us -> 1.53 us
where the time goes in v2:
time: 53.7 us; the launch traced here: 53.6 us
  Pallas kernels  51.4 us (96%)
  local copies, waits for them, and re-layouts  1.53 us (3%)
  between operations  0.64 us (1%)
    pallas_call x1, Pallas kernels, per_device(): pl.pallas_call(functools.partial(kernel, nd, nl, steps, pulses, 4), out_s...  51.4 us
    unnamed x2, local copies, waits for them, and re-layouts  1.53 us

profile of v2, /device:TPU:33, one launch (start us, length us, event | category | flops | bytes accessed | tf_op | source)
XLA Modules:
  0.0 53.6 jit_solution(11556651434137152354)
XLA Ops:
  0.6 51.4 %shard_map.95 = (f32[9,8,16,256]{3,2,1,0:T(8,128)S(1)}, f32[1,64]{1,0:T(1,128)S(1)}) custom-call(f32[9,8,16,256]{3,2,1,0:T(8,128)} %cp_in.1, f32[9,8,16,256]{3,2,1,0:T(8,128)} %ec_in.1, f32[8,16,256]{2,1,0:T(8,128)} %bu_in.1, f32[2,8,16,256]{3,2,1,0:T(8,128)} %mo_in.1, f32[8,16,256]{2,1,0:T(8,128)} %yi_in.1, s32[3,8,16,256]{3,2,1,0:T(8,128)} %ma_in.1, ...), custom_call_target="tpu_custom_call" | custom-call | tf_op jit(solution)/shard_map/pallas_call | solution.py:935
  52.1 1.0 %copy.12 = f32[9,8,16,256]{3,2,1,0:T(8,128)} copy(f32[9,8,16,256]{3,2,1,0:T(8,128)S(1)} %get-tuple-element.6) | data formatting | bytes 2359296
  53.1 0.5 copy.13

commit v3 on v2

--- a/solution.py
+++ b/solution.py
@@ -159,15 +159,15 @@
 
 
 def kernel(
-    nd, nl, steps, pulses, wide_y,
+    nd, nl, steps, pulses,
     cp_in, ec_in, bu_in, mo_in, yi_in, ma_in, fp_in, amp_in,
     out_ref, pulse_ref,
     cp, ec, bu, mo, yi, ma, fp_ref, amp_ref,
     st, sp, co, vs, vb, hist, cf, gy,
     load_map, q_map, fx_send, fx_low, fx_high, zs_low, zs_high, zc_low, zc_high, zm_low, zm_high,
     vx_send, vx_low, vx_high, cor_send, cor_recv,
-    psum_buf, ysum_buf, xsum_buf, total_buf,
-    in_sem, send_sem, recv_sem, far_sem,
+    psum_buf, sums_buf, total_buf,
+    in_sem, send_sem, recv_sem, far_sem, lat_sem,
 ):
     d = lax.axis_index("depth")
     l = lax.axis_index("lat")
@@ -199,25 +199,10 @@
     @pl.when(has_low)
     def _():
         greet(d, low)
-        greet(up, low)
-        greet(down, low)
 
     @pl.when(has_high)
     def _():
         greet(d, high)
-        greet(up, high)
-        greet(down, high)
-
-    l_y = lax.rem(l, wide_y)
-    l_x = l // wide_y
-    n_x = nl // wide_y
-    y_peers = [l_x * wide_y + lax.rem(l_y + k, wide_y) for k in range(1, wide_y)]
-    x_peers = [lax.rem(l_x + k, n_x) * wide_y + l_y for k in range(1, n_x)]
-
-    @pl.when(top)
-    def _():
-        for peer in y_peers + x_peers:
-            greet(d, peer)
 
     others = ((mo_in, mo), (yi_in, yi), (ma_in, ma), (fp_in, fp_ref), (amp_in, amp_ref), (bu_in, bu), (ec_in, ec))
     static_in = [load_in(1 + k, source, target) for k, (source, target) in enumerate(others[:5])]
@@ -252,22 +237,24 @@
             for h in range(2):
                 fx_send[side, 2 * k + h] = face(st, order[k], x, h)
 
-    near = 2 + 3 * has_low.astype(jnp.int32) + 3 * has_high.astype(jnp.int32)
-    pl.semaphore_wait(barrier, near + top.astype(jnp.int32) * (len(y_peers) + len(x_peers)))
+    pl.semaphore_wait(barrier, 2 + has_low.astype(jnp.int32) + has_high.astype(jnp.int32))
 
     class Exchange:
         def __init__(self):
             self.depth, self.low, self.high = [], [], []
 
-        def start(self):
+        def start(self, more=None):
+            more_low = more.low if more else []
+            more_high = more.high if more else []
+
             @pl.when(has_low)
             def _():
-                for copy in self.low:
+                for copy in self.low + more_low:
                     copy.start()
 
             @pl.when(has_high)
             def _():
-                for copy in self.high:
+                for copy in self.high + more_high:
                     copy.start()
 
             for copy in self.depth:
@@ -438,7 +425,7 @@
         for ref, field, place, value in later:
             ref[field, place, :] = value
 
-    def everywhere(unit):
+    def everywhere(unit, take_corners):
         def inner(z, carry):
             later = []
             for t in range(2):
@@ -447,6 +434,8 @@
             return carry
 
         lax.fori_loop(0, NZ_OWN, inner, 0, unroll=UNROLL_S)
+
+        take_corners()
 
         def outer(side, carry):
             z = -1 + (NZ_OWN + 1) * side
@@ -469,7 +458,7 @@
     def coefficients(tile, n):
         return [tile.load(cf, k) for k in (0, 1, 2, 3 + n)]
 
-    def forward_stress(n):
+    def forward_stress(n, take_corners):
         v = vs.at[n]
         record = hist.at[n]
 
@@ -490,7 +479,7 @@
                 tile.store(later, record, 6, h, factor)
                 tile.store(later, record, 7, h, slope)
 
-        everywhere(unit)
+        everywhere(unit, take_corners)
 
         @pl.when(top)
         def _():
@@ -499,7 +488,7 @@
                     place = pl.ds(row_of(0, x, h), count)
                     st[2, place, :] += gains[n] * load_map[pl.ds(BASE + GROUP * h + x, count), :]
 
-    def turn():
+    def turn(take_corners):
         n = steps - 1
         v = vs.at[n]
 
@@ -517,9 +506,9 @@
                     tile.store(later, sp, k, h, stress[k])
                     tile.store(later, co, k, h, keep(inside, strain[k]))
 
-        everywhere(unit)
-
-    def backward_stress(n):
+        everywhere(unit, take_corners)
+
+    def backward_stress(n, take_corners):
         w = vs.at[2 * steps - 2 - n]
         record = hist.at[n]
 
@@ -537,7 +526,7 @@
                     tile.store(later, sp, k, h, stress[k])
                     tile.store(later, co, k, h, keep(inside, strain[k]))
 
-        everywhere(unit)
+        everywhere(unit, take_corners)
 
     def forward_velocity(n):
         def body(z, carry):
@@ -585,7 +574,7 @@
         v = vs.at[p]
         wide = p < 2 * steps - 1
         to_low, to_high = (WIDE_LOW, WIDE_HIGH) if wide else (THIN_LOW, THIN_HIGH)
-        step = Exchange()
+        step, corners = Exchange(), Exchange()
 
         def layers(field, count, z, depth):
             return v.at[pl.ds(field, count), pl.ds(row_of(z, 0), depth * LAYER), :]
@@ -613,20 +602,20 @@
                 for field in corner_fields[c]:
                     for h in range(2):
                         cor_send[p, c, pl.ds(2 * field + h, 1), :] = v[field, pl.ds(row_of(z, x, h), 1), :]
-            step.high = [
+            corners.high = [
                 remote(cor_send.at[p, 0], cor_recv.at[p, 0], (down, high)),
                 remote(cor_send.at[p, 1], cor_recv.at[p, 1], (up, high)),
             ]
-            step.low = [
+            corners.low = [
                 remote(cor_send.at[p, 2], cor_recv.at[p, 2], (down, low)),
                 remote(cor_send.at[p, 3], cor_recv.at[p, 3], (up, low)),
             ]
         count = 2 * len(to_low)
-        step.low.insert(0, remote(vx_send.at[p, 0, pl.ds(0, count)], vx_high.at[p, pl.ds(0, count)], (d, low)))
+        step.low.append(remote(vx_send.at[p, 0, pl.ds(0, count)], vx_high.at[p, pl.ds(0, count)], (d, low)))
         count = 2 * len(to_high)
-        step.high.insert(0, remote(vx_send.at[p, 1, pl.ds(0, count)], vx_low.at[p, pl.ds(0, count)], (d, high)))
-        step.start()
-        return step
+        step.high.append(remote(vx_send.at[p, 1, pl.ds(0, count)], vx_low.at[p, pl.ds(0, count)], (d, high)))
+        step.start(corners)
+        return step, corners
 
     def own_y_differences(p):
         v = vs.at[p]
@@ -645,11 +634,14 @@
         lax.fori_loop(0, NZ_OWN, body, 0, unroll=2)
 
     def take_velocity(p, step):
+        step, corners = step
         own_y_differences(p)
         v = vs.at[p]
         wide = p < 2 * steps - 1
         to_low, to_high = (WIDE_LOW, WIDE_HIGH) if wide else (THIN_LOW, THIN_HIGH)
         step.wait_send()
+        if wide:
+            corners.wait_send()
         step.wait_recv()
 
         def clear(field, z, depth):
@@ -681,7 +673,8 @@
         for k, (field, here, there) in enumerate(to_high):
             for h in range(2):
                 put_face(v, field, there, h, vx_low[p, 2 * k + h])
-        if wide:
+        def take_corners():
+            corners.wait_recv()
             for c, (x, z, outside) in enumerate(
                 ((-1, -1, top), (-1, NZ_OWN, bottom), (NX_OWN, -1, top), (NX_OWN, NZ_OWN, bottom))
             ):
@@ -690,6 +683,8 @@
                         value = cor_recv[p, c, pl.ds(2 * field + h, 1), :]
                         v[field, pl.ds(row_of(z, x, h), 1), :] = jnp.where(outside, 0.0, value)
 
+        return take_corners
+
     rounds = []
     reach = 2
     while reach < nd // 2:
@@ -701,10 +696,26 @@
             for way, other in enumerate((lax.rem(d + rounds[i], nd), lax.rem(d + nd - rounds[i], nd))):
                 pl.semaphore_signal(far_sem.at[2 * i + way], inc=1, device_id=(other, l), device_id_type=MESH)
 
+            @pl.when(jnp.logical_and(top, l + rounds[i] < nl))
+            def _():
+                pl.semaphore_signal(lat_sem.at[2 * i], inc=1, device_id=(d, l + rounds[i]), device_id_type=MESH)
+
+            @pl.when(jnp.logical_and(top, l >= rounds[i]))
+            def _():
+                pl.semaphore_signal(lat_sem.at[2 * i + 1], inc=1, device_id=(d, l - rounds[i]), device_id_type=MESH)
+
     def far_wait(i):
         if i < len(rounds):
             for way in range(2):
                 pl.semaphore_wait(far_sem.at[2 * i + way], 1)
+
+            @pl.when(jnp.logical_and(top, l >= rounds[i]))
+            def _():
+                pl.semaphore_wait(lat_sem.at[2 * i], 1)
+
+            @pl.when(jnp.logical_and(top, l + rounds[i] < nl))
+            def _():
+                pl.semaphore_wait(lat_sem.at[2 * i + 1], 1)
 
     def note_surface(gain, w_slot, start):
         @pl.when(top)
@@ -719,8 +730,7 @@
                     spot = pl.ds(16 * h + 8 * t, 8)
                     q_map[spot, :] = gain * value if start else q_map[spot, :] + gain * value
 
-    y_copies = [remote(psum_buf.at[0], ysum_buf.at[l_y], (d, peer)) for peer in y_peers]
-    x_copies = [remote(psum_buf.at[1], xsum_buf.at[l_x], (d, peer)) for peer in x_peers]
+    peer_copies = [remote(psum_buf, sums_buf.at[l], (d, lax.rem(l + k, nl))) for k in range(1, nl)]
 
     def add_up_pulses():
         @pl.when(top)
@@ -741,75 +751,46 @@
                 jnp.ones((8, 128), F32), total, (((1,), (1,)), ((), ())),
                 precision=lax.Precision.HIGHEST, preferred_element_type=F32,
             )
-            psum_buf[0] = zero
-            psum_buf[0, :, pl.ds(0, pulses)] = sums
-            for copy in y_copies:
+            psum_buf[...] = zero
+            psum_buf[:, pl.ds(0, pulses)] = sums
+            for copy in peer_copies:
                 copy.start()
-            ysum_buf[l_y] = psum_buf[0]
-            for copy in y_copies:
-                copy.wait_recv()
-            sums = ysum_buf[0]
-            for k in range(1, wide_y):
-                sums = sums + ysum_buf[k]
-            psum_buf[1] = sums
-            for copy in x_copies:
-                copy.start()
-            xsum_buf[l_x] = sums
-            for copy in y_copies:
-                copy.wait_send()
-
-    chips = nd // 2
-    far = sorted(range(1, chips), key=lambda k: -min(k, chips - k))
+            sums_buf[l] = psum_buf[...]
+
+    far = sorted(range(1, nd), key=lambda k: -min(k // 2, nd // 2 - k // 2))
     far_ids = [next(ids) for _ in far]
-    core_id = next(ids)
 
     def spread_copy(k, send_id):
         return pltpu.make_async_remote_copy(
             src_ref=total_buf, dst_ref=total_buf, send_sem=send_sem.at[send_id], recv_sem=recv_sem.at[far_ids[0]],
-            device_id=(2 * k, l), device_id_type=MESH,
+            device_id=(k, l), device_id_type=MESH,
         )
 
-    core_copy = pltpu.make_async_remote_copy(
-        src_ref=total_buf, dst_ref=total_buf, send_sem=send_sem.at[core_id], recv_sem=recv_sem.at[core_id],
-        device_id=(d + 1 - 2 * lax.rem(d, 2), l), device_id_type=MESH,
-    )
     scale = math.sqrt(pulses / (NX_OWN * nl * 256))
 
     def spread_pulses():
         @pl.when(top)
         def _():
-            for copy in x_copies:
+            for copy in peer_copies:
                 copy.wait_recv()
-            sums = xsum_buf[0]
-            for k in range(1, n_x):
-                sums = sums + xsum_buf[k]
+            sums = sums_buf[0]
+            for k in range(1, nl):
+                sums = sums + sums_buf[k]
             total_buf[...] = sums * scale
             for k, send_id in zip(far, far_ids):
                 spread_copy(k, send_id).start()
-            core_copy.start()
-            for copy in x_copies:
-                copy.wait_send()
 
     def finish_pulses():
-        even = lax.rem(d, 2) == 0
-
-        @pl.when(jnp.logical_and(even, jnp.logical_not(top)))
+        @pl.when(jnp.logical_not(top))
         def _():
             spread_copy(1, far_ids[0]).wait_recv()
-            core_copy.start()
-
-        @pl.when(jnp.logical_not(even))
-        def _():
-            core_copy.wait_recv()
 
         pulse_ref[...] = total_buf[pl.ds(0, 1), pl.ds(0, pulses)]
-
-        @pl.when(even)
-        def _():
-            core_copy.wait_send()
 
         @pl.when(top)
         def _():
+            for copy in peer_copies:
+                copy.wait_send()
             for k, send_id in zip(far, far_ids):
                 spread_copy(k, send_id).wait_send()
 
@@ -834,9 +815,9 @@
         load_map[pl.ds(BASE + GROUP * h - 1, 1), :] = fx_low[24, pl.ds(h, 1), :]
         load_map[pl.ds(BASE + GROUP * h + NX_OWN, 1), :] = fx_high[24, pl.ds(h, 1), :]
     for n in range(steps - 1):
-        take_velocity(n, step)
+        take_corners = take_velocity(n, step)
         far_wait(n)
-        forward_stress(n)
+        forward_stress(n, take_corners)
         forward_velocity(n + 1)
         step = send_velocity(n + 1)
         far_signal(n + 1)
@@ -849,9 +830,9 @@
                     put_face(sp, k, -1, h, fx_low[25 + 2 * k + h])
                     put_face(sp, k, NX_OWN, h, fx_high[25 + 2 * k + h])
 
-    take_velocity(steps - 1, step)
+    take_corners = take_velocity(steps - 1, step)
     far_wait(steps - 1)
-    turn()
+    turn(take_corners)
     pulse_sends = []
     for n in range(steps - 1, -1, -1):
         backward_velocity(n)
@@ -863,9 +844,9 @@
             note_surface(gains[n - 1], slot, False)
         if n == 1:
             add_up_pulses()
-        take_velocity(slot, step)
+        take_corners = take_velocity(slot, step)
         if n > 0:
-            backward_stress(n - 1)
+            backward_stress(n - 1, take_corners)
 
     def last_stress(z, carry):
         plain = []
@@ -923,17 +904,17 @@
         vmem((phases, 10) + tile, F32),
         vmem((phases - 1, 4) + tile, F32),
         vmem((phases - 1, 4) + tile, F32),
-        vmem((2,) + tile, F32),
-        vmem((4,) + tile, F32),
-        vmem((4,) + tile, F32),
+        vmem(tile, F32),
+        vmem((nl,) + tile, F32),
         vmem(tile, F32),
         pltpu.SemaphoreType.DMA((9,)),
-        pltpu.SemaphoreType.DMA((112,)),
-        pltpu.SemaphoreType.DMA((112,)),
+        pltpu.SemaphoreType.DMA((128,)),
+        pltpu.SemaphoreType.DMA((128,)),
+        pltpu.SemaphoreType.REGULAR((8,)),
         pltpu.SemaphoreType.REGULAR((8,)),
     ]
     adjoint, sums = pl.pallas_call(
-        functools.partial(kernel, nd, nl, steps, pulses, 4),
+        functools.partial(kernel, nd, nl, steps, pulses),
         out_shape=(
             pltpu.VMEM(checkpoint.shape, F32),
             pltpu.VMEM((1, pulses), F32),

time: 53.7 us -> 49.2 us (0.916)
  Pallas kernels: 51.4 us -> 46.9 us
    pallas_call x1, Pallas kernels: 51.4 us -> 46.9 us  [per_device(): pl.pallas_call(functools.partial(kernel, nd, nl, steps, pulses), out_shap...]
where the time goes in v3:
time: 49.2 us; the launch traced here: 49 us
  Pallas kernels  46.9 us (95%)
  local copies, waits for them, and re-layouts  1.53 us (3%)
  between operations  0.64 us (1%)
    pallas_call x1, Pallas kernels, per_device(): pl.pallas_call(functools.partial(kernel, nd, nl, steps, pulses), out_shap...  46.9 us
    unnamed x2, local copies, waits for them, and re-layouts  1.53 us

profile of v3, /device:TPU:33, one launch (start us, length us, event | category | flops | bytes accessed | tf_op | source)
XLA Modules:
  0.0 49.0 jit_solution(14844853689506666392)
XLA Ops:
  0.6 46.9 %shard_map.95 = (f32[9,8,16,256]{3,2,1,0:T(8,128)S(1)}, f32[1,64]{1,0:T(1,128)S(1)}) custom-call(f32[9,8,16,256]{3,2,1,0:T(8,128)} %cp_in.1, f32[9,8,16,256]{3,2,1,0:T(8,128)} %ec_in.1, f32[8,16,256]{2,1,0:T(8,128)} %bu_in.1, f32[2,8,16,256]{3,2,1,0:T(8,128)} %mo_in.1, f32[8,16,256]{2,1,0:T(8,128)} %yi_in.1, s32[3,8,16,256]{3,2,1,0:T(8,128)} %ma_in.1, ...), custom_call_target="tpu_custom_call" | custom-call | tf_op jit(solution)/shard_map/pallas_call | solution.py:916
  47.5 1.0 %copy.12 = f32[9,8,16,256]{3,2,1,0:T(8,128)} copy(f32[9,8,16,256]{3,2,1,0:T(8,128)S(1)} %get-tuple-element.6) | data formatting | bytes 2359296
  48.5 0.5 %copy.13 = f32[64]{0:T(128)} copy(f32[64]{0:T(128)S(1)} %bitcast.1) | data formatting | bytes 512

commit v4 on v3

--- a/solution.py
+++ b/solution.py
@@ -152,7 +152,7 @@
 
 TO_LOW = (0, 1, 2, 3, 4, 5)
 TO_HIGH = (3, 4, 0, 1, 2, 5)
-WIDE_LOW = ((0, 0, 16), (1, 0, 16), (2, 0, 16), (1, 1, 17), (2, 1, 17))
+WIDE_LOW = ((1, 0, 16), (2, 0, 16), (0, 0, 16), (1, 1, 17), (2, 1, 17))
 WIDE_HIGH = ((0, 15, -1), (1, 15, -1), (2, 15, -1), (0, 14, -2))
 THIN_LOW = ((1, 0, 16), (2, 0, 16))
 THIN_HIGH = ((0, 15, -1),)
@@ -186,7 +186,13 @@
         copy.start()
         return copy
 
-    stress_in = load_in(0, cp_in.at[pl.ds(3, 6)], cp.at[pl.ds(3, 6)])
+    def load_rows(k, field, count, x, rows):
+        part = (pl.ds(field, count), slice(None), pl.ds(x, rows))
+        return load_in(k, cp_in.at[part], cp.at[part])
+
+    low_in = load_rows(0, 3, 1, 0, 8)
+    high_in = load_rows(9, 6, 2, 8, 8)
+    stress_in = [load_rows(10, 7, 2, 0, 8), load_rows(11, 8, 1, 8, 8), load_rows(12, 4, 2, 0, 16), load_rows(13, 3, 1, 8, 8), load_rows(14, 6, 1, 0, 8)]
 
     barrier = pltpu.get_barrier_semaphore()
 
@@ -220,18 +226,23 @@
     def own(z, t, h):
         return (z, pl.ds(8 * t, 8), pl.ds(128 * h, 128))
 
-    def stage_stress(z, carry):
-        for t in range(2):
-            for h in range(2):
-                for k in range(6):
+    first_parts = ((0, 0), (3, 1), (4, 1))
+
+    def stage_parts(parts):
+        def body(z, carry):
+            for k, t in parts:
+                for h in range(2):
                     st[k, pl.ds(row_of(z, 8 * t, h), 8), :] = cp[(3 + k,) + own(z, t, h)]
-        return carry
+            return carry
+
+        lax.fori_loop(0, NZ_OWN, body, 0)
 
     def face(ref, field, x, h):
         return ref[field, pl.ds(row_of(0, x, h), NZ_OWN, LAYER), :]
 
-    stress_in.wait()
-    lax.fori_loop(0, NZ_OWN, stage_stress, 0)
+    low_in.wait()
+    high_in.wait()
+    stage_parts(first_parts)
     for side, order, x, count in ((0, TO_LOW, 0, 1), (1, TO_HIGH, NX_OWN - 1, 2)):
         for k in range(count):
             for h in range(2):
@@ -244,6 +255,10 @@
             self.depth, self.low, self.high = [], [], []
 
         def start(self, more=None):
+            self.start_x(more)
+            self.start_depth(more)
+
+        def start_x(self, more=None):
             more_low = more.low if more else []
             more_high = more.high if more else []
 
@@ -257,7 +272,8 @@
                 for copy in self.high + more_high:
                     copy.start()
 
-            for copy in self.depth:
+        def start_depth(self, more=None):
+            for copy in self.depth + (more.depth if more else []):
                 copy.start()
 
         def wait_send(self):
@@ -296,7 +312,11 @@
     ]
     first_faces.low = [remote(fx_send.at[0, pl.ds(0, 2)], fx_high.at[pl.ds(0, 2)], (d, low))]
     first_faces.high = [remote(fx_send.at[1, pl.ds(0, 4)], fx_low.at[pl.ds(0, 4)], (d, high))]
-    first_faces.start()
+    first_faces.start_x()
+    for copy in stress_in:
+        copy.wait()
+    first_faces.start_depth()
+    stage_parts([(k, t) for k in range(6) for t in range(2) if (k, t) not in first_parts])
     def stage(z, carry):
         for t in range(2):
             for h in range(2):
@@ -576,21 +596,19 @@
         to_low, to_high = (WIDE_LOW, WIDE_HIGH) if wide else (THIN_LOW, THIN_HIGH)
         step, corners = Exchange(), Exchange()
 
-        def layers(field, count, z, depth):
-            return v.at[pl.ds(field, count), pl.ds(row_of(z, 0), depth * LAYER), :]
-
+        def layer(field, count, here, there, where):
+            return [
+                remote(
+                    v.at[pl.ds(field, count), pl.ds(row_of(here, 0), GROUP + NX_OWN), :],
+                    v.at[pl.ds(field, count), pl.ds(row_of(there, 0), GROUP + NX_OWN), :],
+                    where,
+                )
+            ]
+
+        step.depth = layer(2, 1, last, -1, (down, l)) + layer(0, 2, 0, NZ_OWN, (up, l))
         if wide:
-            step.depth = [
-                remote(layers(0, 2, last, 1), layers(0, 2, -1, 1), (down, l)),
-                remote(layers(2, 1, last - 1, 2), layers(2, 1, -2, 2), (down, l)),
-                remote(layers(0, 2, 0, 2), layers(0, 2, NZ_OWN, 2), (up, l)),
-                remote(layers(2, 1, 0, 1), layers(2, 1, NZ_OWN, 1), (up, l)),
-            ]
-        else:
-            step.depth = [
-                remote(layers(2, 1, last, 1), layers(2, 1, -1, 1), (down, l)),
-                remote(layers(0, 2, 0, 1), layers(0, 2, NZ_OWN, 1), (up, l)),
-            ]
+            corners.depth = layer(0, 2, last, -1, (down, l)) + layer(0, 2, 1, NZ_OWN + 1, (up, l))
+            corners.depth += layer(2, 1, last - 1, -2, (down, l)) + layer(2, 1, 0, NZ_OWN, (up, l))
         for k, (field, here, there) in enumerate(to_low):
             for h in range(2):
                 vx_send[p, 0, 2 * k + h] = face(v, field, here, h)
@@ -610,10 +628,16 @@
                 remote(cor_send.at[p, 2], cor_recv.at[p, 2], (down, low)),
                 remote(cor_send.at[p, 3], cor_recv.at[p, 3], (up, low)),
             ]
-        count = 2 * len(to_low)
+        count = 2 * len(THIN_LOW)
         step.low.append(remote(vx_send.at[p, 0, pl.ds(0, count)], vx_high.at[p, pl.ds(0, count)], (d, low)))
-        count = 2 * len(to_high)
+        if wide:
+            span = pl.ds(count, 2 * len(to_low) - count)
+            corners.low.append(remote(vx_send.at[p, 0, span], vx_high.at[p, span], (d, low)))
+        count = 2 * len(THIN_HIGH)
         step.high.append(remote(vx_send.at[p, 1, pl.ds(0, count)], vx_low.at[p, pl.ds(0, count)], (d, high)))
+        if wide:
+            span = pl.ds(count, 2 * len(to_high) - count)
+            corners.high.append(remote(vx_send.at[p, 1, span], vx_low.at[p, span], (d, high)))
         step.start(corners)
         return step, corners
 
@@ -644,37 +668,43 @@
             corners.wait_send()
         step.wait_recv()
 
-        def clear(field, z, depth):
-            def body(i, carry):
-                v[field, pl.ds(row_of(z, 0) + 8 * i, 8), :] = zero
-                return carry
-
-            lax.fori_loop(0, depth * LAYER // 8, body, 0)
+        def clear(*places):
+            for field, z in places:
+                for t in range(2):
+                    for h in range(2):
+                        v[field, pl.ds(row_of(z, 8 * t, h), 8), :] = zero
 
         @pl.when(top)
         def _():
-            if wide:
-                clear(0, -1, 1)
-                clear(1, -1, 1)
-                clear(2, -2, 2)
-            else:
-                clear(2, -1, 1)
+            clear((2, -1))
 
         @pl.when(bottom)
         def _():
-            for field in range(2):
-                clear(field, NZ_OWN, 2 if wide else 1)
-            if wide:
-                clear(2, NZ_OWN, 1)
-
-        for k, (field, here, there) in enumerate(to_low):
-            for h in range(2):
-                put_face(v, field, there, h, vx_high[p, 2 * k + h])
-        for k, (field, here, there) in enumerate(to_high):
-            for h in range(2):
-                put_face(v, field, there, h, vx_low[p, 2 * k + h])
+            clear((0, NZ_OWN), (1, NZ_OWN))
+
+        def put_faces(low_span, high_span):
+            for k in low_span:
+                field, here, there = to_low[k]
+                for h in range(2):
+                    put_face(v, field, there, h, vx_high[p, 2 * k + h])
+            for k in high_span:
+                field, here, there = to_high[k]
+                for h in range(2):
+                    put_face(v, field, there, h, vx_low[p, 2 * k + h])
+
+        put_faces(range(len(THIN_LOW)), range(len(THIN_HIGH)))
         def take_corners():
             corners.wait_recv()
+
+            @pl.when(top)
+            def _():
+                clear((0, -1), (1, -1), (2, -2))
+
+            @pl.when(bottom)
+            def _():
+                clear((0, NZ_OWN + 1), (1, NZ_OWN + 1), (2, NZ_OWN))
+
+            put_faces(range(len(THIN_LOW), len(to_low)), range(len(THIN_HIGH), len(to_high)))
             for c, (x, z, outside) in enumerate(
                 ((-1, -1, top), (-1, NZ_OWN, bottom), (NX_OWN, -1, top), (NX_OWN, NZ_OWN, bottom))
             ):
@@ -907,9 +937,9 @@
         vmem(tile, F32),
         vmem((nl,) + tile, F32),
         vmem(tile, F32),
-        pltpu.SemaphoreType.DMA((9,)),
-        pltpu.SemaphoreType.DMA((128,)),
-        pltpu.SemaphoreType.DMA((128,)),
+        pltpu.SemaphoreType.DMA((15,)),
+        pltpu.SemaphoreType.DMA((176,)),
+        pltpu.SemaphoreType.DMA((176,)),
         pltpu.SemaphoreType.REGULAR((8,)),
         pltpu.SemaphoreType.REGULAR((8,)),
     ]

time: 49.2 us -> 49 us (level)
  no operation moved by 1% of the time
where the time goes in v4:
time: 49 us; the launch traced here: 48.9 us
  Pallas kernels  46.7 us (95%)
  local copies, waits for them, and re-layouts  1.53 us (3%)
  between operations  0.64 us (1%)
    pallas_call x1, Pallas kernels, per_device(): pl.pallas_call(functools.partial(kernel, nd, nl, steps, pulses), out_shap...  46.7 us
    unnamed x2, local copies, waits for them, and re-layouts  1.53 us

profile of v4, /device:TPU:33, one launch (start us, length us, event | category | flops | bytes accessed | tf_op | source)
XLA Modules:
  0.0 48.9 jit_solution(15688358292134158855)
XLA Ops:
  0.6 46.7 %shard_map.95 = (f32[9,8,16,256]{3,2,1,0:T(8,128)S(1)}, f32[1,64]{1,0:T(1,128)S(1)}) custom-call(f32[9,8,16,256]{3,2,1,0:T(8,128)} %cp_in.1, f32[9,8,16,256]{3,2,1,0:T(8,128)} %ec_in.1, f32[8,16,256]{2,1,0:T(8,128)} %bu_in.1, f32[2,8,16,256]{3,2,1,0:T(8,128)} %mo_in.1, f32[8,16,256]{2,1,0:T(8,128)} %yi_in.1, s32[3,8,16,256]{3,2,1,0:T(8,128)} %ma_in.1, ...), custom_call_target="tpu_custom_call" | custom-call | tf_op jit(solution)/shard_map/pallas_call | solution.py:946
  47.3 1.0 %copy.12 = f32[9,8,16,256]{3,2,1,0:T(8,128)} copy(f32[9,8,16,256]{3,2,1,0:T(8,128)S(1)} %get-tuple-element.6) | data formatting | bytes 2359296
  48.3 0.5 %copy.13 = f32[64]{0:T(128)} copy(f32[64]{0:T(128)S(1)} %bitcast.1) | data formatting | bytes 512
